TPU v7x, 128 devices: a whole 4x4x4 slice. The times are simulated.
128 devices in a mesh: fsdp: 128 (over y, z, x, core).
Axes of the slice: x: 4, y: 4, z: 4, core: 2. Of those that a mesh axis runs over, the one named last changes fastest.
Arguments:
- tokens: bfloat16 [16384, 896], P('fsdp'), may hold values from -6 to 6
- cotangent: bfloat16 [16384, 896], P('fsdp'), may hold values from -6 to 6
- lengths: int32 [6], replicated, may hold values from 1 to 8192, 16384 in all
- in_weight: float32 [896, 1152], P('fsdp'), may hold values from -0.1875 to 0.1875
- out_weight: float32 [896, 896], P(None, 'fsdp'), may hold values from -2.5 to 2.5
- gate_weight: float32 [896, 9728], P('fsdp'), may hold values from -0.1875 to 0.1875
- down_weight: float32 [4864, 896], P('fsdp'), may hold values from -0.078125 to 0.078125
- gains: float32 [2, 896], P(None, 'fsdp'), may hold values from 0.8 to 2.7
- in_first: float32 [896, 1152], P('fsdp'), may hold values from -0.000397325 to 0.000397325
- out_first: float32 [896, 896], P(None, 'fsdp'), may hold values from -1.8996278e-05 to 1.8996278e-05
- gate_first: float32 [896, 9728], P('fsdp'), may hold values from -4.98599e-05 to 4.98599e-05
- down_first: float32 [4864, 896], P('fsdp'), may hold values from -0.00012207072 to 0.00012207072
- gains_first: float32 [2, 896], P(None, 'fsdp'), may hold values from -0.00028977904 to 0.00028977904
- in_second: float32 [896, 1152], P('fsdp'), may hold values from 1.6607624e-08 to 6.63042e-08
- out_second: float32 [896, 896], P(None, 'fsdp'), may hold values from 3.7962317e-11 to 1.5156058e-10
- gate_second: float32 [896, 9728], P('fsdp'), may hold values from 2.6152822e-10 to 1.0441241e-09
- down_second: float32 [4864, 896], P('fsdp'), may hold values from 1.5676126e-09 to 6.2585297e-09
- gains_second: float32 [2, 896], P(None, 'fsdp'), may hold values from 8.833842e-09 to 3.526819e-08
Outputs:
- output: bfloat16 [16384, 896], P('fsdp')
- input_grad: bfloat16 [16384, 896], P('fsdp')
- in_master: float32 [896, 1152], P('fsdp')
- in_moment: float32 [896, 1152], P('fsdp')
- in_square: float32 [896, 1152], P('fsdp')
- in_copy: bfloat16 [896, 1152], P('fsdp')
- out_master: float32 [896, 896], P(None, 'fsdp')
- out_moment: float32 [896, 896], P(None, 'fsdp')
- out_square: float32 [896, 896], P(None, 'fsdp')
- out_copy: bfloat16 [896, 896], P(None, 'fsdp')
- gate_master: float32 [896, 9728], P('fsdp')
- gate_moment: float32 [896, 9728], P('fsdp')
- gate_square: float32 [896, 9728], P('fsdp')
- gate_copy: bfloat16 [896, 9728], P('fsdp')
- down_master: float32 [4864, 896], P('fsdp')
- down_moment: float32 [4864, 896], P('fsdp')
- down_square: float32 [4864, 896], P('fsdp')
- down_copy: bfloat16 [4864, 896], P('fsdp')
- gains_master: float32 [2, 896], P(None, 'fsdp')
- gains_moment: float32 [2, 896], P(None, 'fsdp')
- gains_square: float32 [2, 896], P(None, 'fsdp')
- gains_copy: bfloat16 [2, 896], P(None, 'fsdp')
- grad_norm: float32 [], replicated
Inputs may be any that keep to these rules, and one draw needn't show every extreme that they name: The 6 lengths sum to 16384, and the longest is exactly 8192.
All inputs are finite; a program needn't handle non-finite values.
Results may differ from a plain program's by a relative error of at most 0.019.
The roundings to bfloat16 on the way count: a program that leaves them out, or rounds other values in their place, can miss the bound.
Values may be sent and summed in bfloat16 or wider, within the bound.
A program may use at most 320 MiB of HBM per device.

v0:
```python
import jax
import jax.numpy as jnp
from jax import lax
from jax.sharding import PartitionSpec as P

D = 896
FF = 4864
HEADS = 14
KV_HEADS = 2
HEAD_DIM = 64
DOC_DEV = 64
STEP = 10


norm_eps = 1e-05
rope_base = 130000.0
beta_first = 0.9
beta_second = 0.95
adam_eps = 1e-08
decay_rate = 0.1
matrix_rate = 4.0
gain_rate = 1.5
masked_score = -1e30
query_block = 32


def rms_norm(values, gain_row):
    scale_rows = lax.rsqrt(jnp.mean(values * values, axis=-1, keepdims=True) + norm_eps)
    return values * scale_rows * gain_row


def rotate(values, cosine, sine):
    middle = values.shape[-1] // 2
    turned = jnp.concatenate([-values[..., middle:], values[..., :middle]], axis=-1)
    return values * cosine + turned * sine


def unrotate(values, cosine, sine):
    middle = values.shape[-1] // 2
    spun = values * sine
    turned = jnp.concatenate([spun[..., middle:], -spun[..., :middle]], axis=-1)
    return values * cosine + turned


def locate(position, lengths):
    doc_ends = jnp.cumsum(lengths)
    starts = doc_ends - lengths
    inside = (position[:, None] >= starts[None, :]) & (position[:, None] < doc_ends[None, :])
    number = jnp.arange(lengths.shape[0], dtype=jnp.int32)
    document = jnp.sum(jnp.where(inside, number[None, :], 0), axis=1)
    offset = jnp.sum(jnp.where(inside, starts[None, :], 0), axis=1)
    return (document, position - offset)


def rotation_table(doc_place):
    half_dim = HEAD_DIM // 2
    inverse = rope_base ** (-(jnp.arange(half_dim, dtype=jnp.float32) * 2.0) / HEAD_DIM)
    angles = doc_place.astype(jnp.float32)[:, None] * inverse[None, :]
    angles = jnp.concatenate([angles, angles], axis=1)
    return (jnp.cos(angles)[:, None, :], jnp.sin(angles)[:, None, :])


def gate_apply(gate_both):
    half_width = gate_both.shape[1] // 2
    gate_part = gate_both[:, :half_width]
    return gate_part / (1.0 + jnp.exp(-gate_part)) * gate_both[:, half_width:]


def pad_rows(gathered, devices, reach_rows):
    shaped = gathered.reshape(devices, gathered.shape[0] // devices, gathered.shape[1])
    return jnp.pad(shaped, ((0, 0), (reach_rows, 0), (0, 0)))


def window_scores(
    block_query,
    key_pad,
    value_pad,
    first_row,
    reach_rows,
    devices,
    pad_pos,
    pad_doc,
    pad_use,
    block_pos,
    block_doc,
):
    span_rows = query_block + reach_rows
    position = lax.dynamic_slice_in_dim(pad_pos, first_row, span_rows, 1).reshape(-1)
    document = lax.dynamic_slice_in_dim(pad_doc, first_row, span_rows, 1).reshape(-1)
    usable = lax.dynamic_slice_in_dim(pad_use, first_row, span_rows, 1).reshape(-1)
    key_window = lax.dynamic_slice_in_dim(key_pad, first_row, span_rows, 1).reshape(
        devices * span_rows, KV_HEADS, HEAD_DIM
    )
    value_window = lax.dynamic_slice_in_dim(value_pad, first_row, span_rows, 1).reshape(
        devices * span_rows, KV_HEADS, HEAD_DIM
    )
    allowed = (
        usable[None, :]
        & (document[None, :] == block_doc[:, None])
        & (position[None, :] <= block_pos[:, None])
    )
    raw_scores = jnp.einsum(
        "qkgd,skd->kgqs", block_query, key_window, preferred_element_type=jnp.float32
    )
    scores = jnp.where(allowed[None, None], raw_scores * HEAD_DIM ** (-0.5), masked_score)
    return (scores, key_window, value_window)


def adam_step(weight, gradient, moment, square, factor, step_rate):
    gradient = gradient * factor
    moment = beta_first * moment + (1.0 - beta_first) * gradient
    square = beta_second * square + (1.0 - beta_second) * gradient * gradient
    moment_hat = moment / (1.0 - beta_first**STEP)
    square_hat = square / (1.0 - beta_second**STEP)
    updated = weight - step_rate * (
        moment_hat / (jnp.sqrt(square_hat) + adam_eps) + decay_rate * weight
    )
    return (updated, moment, square, updated.astype(jnp.bfloat16))


def body(
    tokens,
    cotangent,
    lengths,
    in_weight,
    out_weight,
    gate_weight,
    down_weight,
    gains,
    in_first,
    out_first,
    gate_first,
    down_first,
    gains_first,
    in_second,
    out_second,
    gate_second,
    down_second,
    gains_second,
):
    devices = lax.axis_size("fsdp")
    device_index = lax.axis_index("fsdp")
    local_rows = tokens.shape[0]
    model_width = tokens.shape[1]
    stride_rows = local_rows // devices
    group_size = HEADS // KV_HEADS
    query_width = HEADS * HEAD_DIM
    key_width = KV_HEADS * HEAD_DIM
    reach_rows = DOC_DEV + 1
    span_rows = query_block + reach_rows
    blocks = local_rows // query_block
    out_divisor = max(1, query_width * 6 // min(DOC_DEV * devices, 1024))
    arrived = (
        lax.all_to_all(
            tokens.reshape(stride_rows, devices, model_width),
            "fsdp",
            split_axis=1,
            concat_axis=0,
            tiled=True,
        ),
        lax.all_to_all(
            cotangent.reshape(stride_rows, devices, model_width),
            "fsdp",
            split_axis=1,
            concat_axis=0,
            tiled=True,
        ),
    )
    inputs = arrived[0].reshape(local_rows, model_width).astype(jnp.float32)
    upstream = arrived[1].reshape(local_rows, model_width)
    position = jnp.arange(local_rows, dtype=jnp.int32) * devices + device_index
    document, doc_place = locate(position, lengths)
    cosine, sine = rotation_table(doc_place)
    pad_local = jnp.arange(local_rows + reach_rows, dtype=jnp.int32) - reach_rows
    owners = jnp.arange(devices, dtype=jnp.int32)
    pad_pos = pad_local[None, :] * devices + owners[:, None]
    pad_use = jnp.broadcast_to(pad_local[None, :] >= 0, pad_pos.shape)
    pad_doc = locate(jnp.maximum(pad_pos, 0).reshape(-1), lengths)[0].reshape(pad_pos.shape)
    in_full, out_full, gains_full = (
        lax.all_gather(in_weight.astype(jnp.bfloat16), "fsdp", axis=0, tiled=True),
        lax.all_gather(out_weight.astype(jnp.bfloat16), "fsdp", axis=1, tiled=True),
        lax.all_gather(gains.astype(jnp.bfloat16), "fsdp", axis=1, tiled=True),
    )
    gain_rows = gains_full.astype(jnp.float32)
    normed = rms_norm(inputs, gain_rows[0]).astype(jnp.bfloat16)
    joined = jnp.dot(normed, in_full, preferred_element_type=jnp.float32)
    queries = rotate(
        joined[:, :query_width].reshape(local_rows, HEADS, HEAD_DIM), cosine, sine
    ).astype(jnp.bfloat16)
    key_rows = (
        rotate(
            joined[:, query_width : query_width + key_width].reshape(
                local_rows, KV_HEADS, HEAD_DIM
            ),
            cosine,
            sine,
        )
        .astype(jnp.bfloat16)
        .reshape(local_rows, key_width)
    )
    value_rows = joined[:, query_width + key_width :].astype(jnp.bfloat16)
    key_all, value_all = (
        lax.all_gather(key_rows, "fsdp", axis=0, tiled=True),
        lax.all_gather(value_rows, "fsdp", axis=0, tiled=True),
    )
    key_pad = pad_rows(key_all, devices, reach_rows)
    value_pad = pad_rows(value_all, devices, reach_rows)
    grouped = queries.reshape(local_rows, KV_HEADS, group_size, HEAD_DIM)

    def attend_step(unused, number):
        first_row = number * query_block
        block_query = lax.dynamic_slice_in_dim(grouped, first_row, query_block, 0)
        block_pos = lax.dynamic_slice_in_dim(position, first_row, query_block, 0)
        block_doc = lax.dynamic_slice_in_dim(document, first_row, query_block, 0)
        scores, key_window, value_window = window_scores(
            block_query,
            key_pad,
            value_pad,
            first_row,
            reach_rows,
            devices,
            pad_pos,
            pad_doc,
            pad_use,
            block_pos,
            block_doc,
        )
        highest_score = jnp.max(scores, axis=-1, keepdims=True)
        log_total = highest_score + jnp.log(
            jnp.sum(jnp.exp(scores - highest_score), axis=-1, keepdims=True)
        )
        weights = jnp.exp(scores - log_total)
        mixed_block = jnp.einsum(
            "kgqs,skd->qkgd",
            weights.astype(jnp.bfloat16),
            value_window,
            preferred_element_type=jnp.float32,
        )
        return (unused, (mixed_block, log_total))

    scanned = lax.scan(attend_step, jnp.zeros((), jnp.float32), jnp.arange(blocks, dtype=jnp.int32))
    mixed_blocks, totals = scanned[1]
    mixed = mixed_blocks.reshape(local_rows, query_width).astype(jnp.bfloat16)
    middle = inputs + jnp.dot(mixed, out_full, preferred_element_type=jnp.float32)
    normed_two = rms_norm(middle, gain_rows[1]).astype(jnp.bfloat16)
    gate_full, down_full = (
        lax.all_gather(gate_weight.astype(jnp.bfloat16), "fsdp", axis=0, tiled=True),
        lax.all_gather(down_weight.astype(jnp.bfloat16), "fsdp", axis=0, tiled=True),
    )
    gate_both = jnp.dot(normed_two, gate_full, preferred_element_type=jnp.float32)
    hidden = gate_apply(gate_both).astype(jnp.bfloat16)
    result = (middle + jnp.dot(hidden, down_full, preferred_element_type=jnp.float32)).astype(
        jnp.bfloat16
    )
    back_gate, back_down, back_gains = (
        lax.all_gather(gate_weight.astype(jnp.bfloat16), "fsdp", axis=0, tiled=True),
        lax.all_gather(down_weight.astype(jnp.bfloat16), "fsdp", axis=0, tiled=True),
        lax.all_gather(gains.astype(jnp.bfloat16), "fsdp", axis=1, tiled=True),
    )
    back_rows = back_gains.astype(jnp.float32)
    delta_hidden = jnp.einsum("td,fd->tf", upstream, back_down, preferred_element_type=jnp.float32)
    delta_gate = jax.vjp(gate_apply, gate_both)[1](delta_hidden)[0].astype(jnp.bfloat16)
    delta_second = jnp.einsum(
        "tf,df->td", delta_gate, back_gate, preferred_element_type=jnp.float32
    )
    middle_part, second_gain = jax.vjp(rms_norm, middle, back_rows[1])[1](delta_second)
    delta_middle = upstream.astype(jnp.float32) + middle_part
    grad_down = jnp.einsum("tf,td->fd", hidden, upstream, preferred_element_type=jnp.float32)
    grad_gate = jnp.einsum("td,tf->df", normed_two, delta_gate, preferred_element_type=jnp.float32)
    feed_sums = (
        lax.psum_scatter(grad_gate, "fsdp", scatter_dimension=0, tiled=True),
        lax.psum_scatter(grad_down, "fsdp", scatter_dimension=0, tiled=True),
    )
    gate_sum, down_sum = (feed_sums[0], feed_sums[1])
    in_back, out_back = (
        lax.all_gather(in_weight.astype(jnp.bfloat16), "fsdp", axis=0, tiled=True),
        lax.all_gather(out_weight.astype(jnp.bfloat16), "fsdp", axis=1, tiled=True),
    )
    delta_branch = delta_middle.astype(jnp.bfloat16)
    grad_out = jnp.einsum("tq,td->qd", mixed, delta_branch, preferred_element_type=jnp.float32)
    delta_mixed = jnp.einsum(
        "td,qd->tq", delta_branch, out_back, preferred_element_type=jnp.float32
    ).astype(jnp.bfloat16)
    back_keys, back_values = (
        lax.all_gather(key_rows, "fsdp", axis=0, tiled=True),
        lax.all_gather(value_rows, "fsdp", axis=0, tiled=True),
    )
    key_again = pad_rows(back_keys, devices, reach_rows)
    value_again = pad_rows(back_values, devices, reach_rows)
    delta_grouped = delta_mixed.reshape(blocks, query_block, KV_HEADS, group_size, HEAD_DIM)

    def back_step(pad_grads, slices):
        number, delta_block, log_total = slices
        first_row = number * query_block
        block_query = lax.dynamic_slice_in_dim(grouped, first_row, query_block, 0)
        block_pos = lax.dynamic_slice_in_dim(position, first_row, query_block, 0)
        block_doc = lax.dynamic_slice_in_dim(document, first_row, query_block, 0)
        scores, key_window, value_window = window_scores(
            block_query,
            key_again,
            value_again,
            first_row,
            reach_rows,
            devices,
            pad_pos,
            pad_doc,
            pad_use,
            block_pos,
            block_doc,
        )
        weights = jnp.exp(scores - log_total)
        delta_weights = jnp.einsum(
            "qkgd,skd->kgqs", delta_block, value_window, preferred_element_type=jnp.float32
        )
        inner = jnp.sum(weights * delta_weights, axis=-1, keepdims=True)
        delta_raw = (weights * (delta_weights - inner) * HEAD_DIM ** (-0.5)).astype(jnp.bfloat16)
        query_part = jnp.einsum(
            "kgqs,skd->qkgd", delta_raw, key_window, preferred_element_type=jnp.float32
        )
        key_part = jnp.einsum(
            "kgqs,qkgd->skd", delta_raw, block_query, preferred_element_type=jnp.float32
        )
        value_part = jnp.einsum(
            "kgqs,qkgd->skd",
            weights.astype(jnp.bfloat16),
            delta_block,
            preferred_element_type=jnp.float32,
        )
        both_parts = jnp.concatenate(
            [
                key_part.reshape(devices, span_rows, key_width),
                value_part.reshape(devices, span_rows, key_width),
            ],
            axis=2,
        )
        current = lax.dynamic_slice_in_dim(pad_grads, first_row, span_rows, 1)
        pad_grads = lax.dynamic_update_slice_in_dim(pad_grads, current + both_parts, first_row, 1)
        return (pad_grads, query_part)

    start_grads = jnp.zeros((devices, local_rows + reach_rows, 2 * key_width), jnp.float32)
    walked = lax.scan(
        back_step, start_grads, (jnp.arange(blocks, dtype=jnp.int32), delta_grouped, totals)
    )
    pad_grads, query_parts = walked
    key_sums = lax.psum_scatter(
        pad_grads[:, reach_rows:, :].reshape(devices * local_rows, 2 * key_width),
        "fsdp",
        scatter_dimension=0,
        tiled=True,
    )
    delta_query = unrotate(query_parts.reshape(local_rows, HEADS, HEAD_DIM), cosine, sine).reshape(
        local_rows, query_width
    )
    delta_key = unrotate(
        key_sums[:, :key_width].reshape(local_rows, KV_HEADS, HEAD_DIM), cosine, sine
    ).reshape(local_rows, key_width)
    delta_joined = jnp.concatenate(
        [delta_query, delta_key, key_sums[:, key_width:]], axis=1
    ).astype(jnp.bfloat16)
    grad_in = jnp.einsum("td,tf->df", normed, delta_joined, preferred_element_type=jnp.float32)
    delta_normed = jnp.einsum(
        "tf,df->td", delta_joined, in_back, preferred_element_type=jnp.float32
    )
    inputs_part, first_gain = jax.vjp(rms_norm, inputs, back_rows[0])[1](delta_normed)
    input_grad = (delta_middle + inputs_part).astype(jnp.bfloat16)
    grad_gains = jnp.stack([first_gain, second_gain])
    attend_sums = (
        lax.psum_scatter(grad_in, "fsdp", scatter_dimension=0, tiled=True),
        lax.psum_scatter(grad_out, "fsdp", scatter_dimension=1, tiled=True),
        lax.psum_scatter(grad_gains, "fsdp", scatter_dimension=1, tiled=True),
    )
    shards = (attend_sums[0], attend_sums[1], gate_sum, down_sum, attend_sums[2])
    local_square = sum((jnp.sum(shard_grad * shard_grad) for shard_grad in shards))
    grad_norm = jnp.sqrt(lax.psum(local_square, "fsdp"))
    factor = 1.0 / jnp.maximum(grad_norm, 1.0)
    in_new = adam_step(
        in_weight, attend_sums[0], in_first, in_second, factor, matrix_rate * D ** (-0.5)
    )
    out_new = adam_step(
        out_weight,
        attend_sums[1],
        out_first,
        out_second,
        factor,
        matrix_rate * out_divisor ** (-0.5),
    )
    gate_new = adam_step(
        gate_weight, gate_sum, gate_first, gate_second, factor, matrix_rate * D ** (-0.5)
    )
    down_new = adam_step(
        down_weight, down_sum, down_first, down_second, factor, matrix_rate * FF ** (-0.5)
    )
    gains_new = adam_step(gains, attend_sums[2], gains_first, gains_second, factor, gain_rate)
    returned = (
        lax.all_to_all(
            result.reshape(local_rows, 1, model_width),
            "fsdp",
            split_axis=0,
            concat_axis=1,
            tiled=True,
        ),
        lax.all_to_all(
            input_grad.reshape(local_rows, 1, model_width),
            "fsdp",
            split_axis=0,
            concat_axis=1,
            tiled=True,
        ),
    )
    output = returned[0].reshape(local_rows, model_width)
    input_back = returned[1].reshape(local_rows, model_width)
    return (
        output,
        input_back,
        in_new[0],
        in_new[1],
        in_new[2],
        in_new[3],
        out_new[0],
        out_new[1],
        out_new[2],
        out_new[3],
        gate_new[0],
        gate_new[1],
        gate_new[2],
        gate_new[3],
        down_new[0],
        down_new[1],
        down_new[2],
        down_new[3],
        gains_new[0],
        gains_new[1],
        gains_new[2],
        gains_new[3],
        grad_norm,
    )


def solution(mesh):
    placed = (
        P("fsdp", None),
        P("fsdp", None),
        P(),
        P("fsdp", None),
        P(None, "fsdp"),
        P("fsdp", None),
        P("fsdp", None),
        P(None, "fsdp"),
        P("fsdp", None),
        P(None, "fsdp"),
        P("fsdp", None),
        P("fsdp", None),
        P(None, "fsdp"),
        P("fsdp", None),
        P(None, "fsdp"),
        P("fsdp", None),
        P("fsdp", None),
        P(None, "fsdp"),
    )
    return jax.shard_map(
        body,
        mesh=mesh,
        in_specs=placed,
        out_specs=(
            P("fsdp", None),
            P("fsdp", None),
            P("fsdp", None),
            P("fsdp", None),
            P("fsdp", None),
            P("fsdp", None),
            P(None, "fsdp"),
            P(None, "fsdp"),
            P(None, "fsdp"),
            P(None, "fsdp"),
            P("fsdp", None),
            P("fsdp", None),
            P("fsdp", None),
            P("fsdp", None),
            P("fsdp", None),
            P("fsdp", None),
            P("fsdp", None),
            P("fsdp", None),
            P(None, "fsdp"),
            P(None, "fsdp"),
            P(None, "fsdp"),
            P(None, "fsdp"),
            P(),
        ),
        check_vma=False,
    )
```

profile of v0, /device:TPU:1, one launch (start us, length us, event | category | flops | bytes accessed | tf_op | source)
XLA Modules:
  0.0 3260.0 jit_solution(1371272446074027359)
XLA Ops:
  27.1 32.6 all-gather
  61.4 19.2 all-gather.16.cloned.1.call-done
  110.1 36.9 %all-gather.18.cloned.1.call-done = bf16[128,7,896]{2,1,0:T(8,128)(2,1)} async-done(((bf16[1,7,896]{2,1,0:T(8,128)(2,1)}), bf16[128,7,896]{2,1,0:T(8,128)(2,1)}) %all-gather.18.cloned.1.call-update) | async-done | bytes 1605648 | tf_op jit(solution)/shard_map/all_gather | solution.py:181
  152.1 62.9 %all-gather.12.cloned.1.call-done = bf16[16384,128]{1,0:T(8,128)(2,1)} async-done(((bf16[128,128]{1,0:T(8,128)(2,1)}), bf16[16384,128]{1,0:T(8,128)(2,1)}) %all-gather.12.cloned.1.call-update) | async-done | bytes 4194320 | tf_op jit(solution)/shard_map/all_gather | solution.py:204
  221.7 61.2 %all-gather.14.cloned.1.call-done = bf16[16384,128]{1,0:T(8,128)(2,1)} async-done(((bf16[128,128]{1,0:T(8,128)(2,1)}), bf16[16384,128]{1,0:T(8,128)(2,1)}) %all-gather.14.cloned.1.call-update) | async-done | bytes 4194320 | tf_op jit(solution)/shard_map/all_gather | solution.py:203
  306.0 275.1 %while.26 = (s32[]{:T(128)}, bf16[4,32,2,7,64]{4,1,3,2,0:T(8,128)(2,1)}, f32[4,2,7,32,1]{3,2,1,4,0:T(8,128)}, s32[4]{0:T(128)}, bf16[128,193,128]{1,0,2:T(8,128)...) while((s32[]{:T(128)}, ...), condition=%wide.region_8.9_spmd.clone, body=%wide.region_5.8_spmd.sunk.clone | while | flops 1464491520 | bytes 112966544 | solution.py:241
  339.6 13.7 fusion.148
  408.1 15.1 fusion.148
  585.0 13.1 reshape.545
  598.0 20.7 reshape.543
  632.1 12.9 multiply_reduce_fusion
  659.0 1003.5 %while.27 = (s32[]{:T(128)}, f32[128,193,256]{1,0,2:T(8,128)}, f32[4,32,2,7,64]{4,1,3,2,0:T(8,128)}, s32[4]{0:T(128)S(1)}, bf16[128,2,7,64]{3,0,2,1:T(8,128)(2,1...) while((s32[]{:T(128)}, f32[128,193,256]{1,0,2:T(8,128)}, ...), condition=%wide.region_13.14_spmd.clone, body=%wide.region_11.13_spmd.sunk.clone | while | flops 3623484928 | bytes 305597856 | solution.py:341
  704.2 15.1 fusion.159
  719.3 14.5 fusion.160
  755.6 15.9 reshape.586
  771.5 15.9 reshape.585
  787.4 23.2 maximum_add_fusion.3
  810.6 80.0 %dynamic_update_slice.28 = f32[128,193,256]{1,0,2:T(8,128)} dynamic-update-slice(f32[128,193,256]{1,0,2:T(8,128)} %get-tuple-element.747, f32[128,97,256]{1,0,2:T(8,128)} %maximum_add_fusion.3, s32[]{:T(128)} %constant.62.clone.1..sunk.3, s32[]{:T(128)S(6)} %select_n.66, s32[]{:T(128)} %constant.62.clone.1..sunk.3) | dynamic-update-slice | bytes 25427972 | tf_op jit(solution)/shard_map/while/body/eval_jaxpr/dynamic_update_slice | solution.py:337
  935.4 15.1 fusion.159
  950.5 14.5 fusion.160
  986.8 15.9 reshape.586
  1002.7 15.9 reshape.585
  1018.6 23.2 maximum_add_fusion.3
  1041.8 106.0 %dynamic_update_slice.28 = f32[128,193,256]{1,0,2:T(8,128)} dynamic-update-slice(f32[128,193,256]{1,0,2:T(8,128)} %get-tuple-element.747, f32[128,97,256]{1,0,2:T(8,128)} %maximum_add_fusion.3, s32[]{:T(128)} %constant.62.clone.1..sunk.3, s32[]{:T(128)S(6)} %select_n.66, s32[]{:T(128)} %constant.62.clone.1..sunk.3) | dynamic-update-slice | bytes 25427972 | tf_op jit(solution)/shard_map/while/body/eval_jaxpr/dynamic_update_slice | solution.py:337
  1192.6 15.1 fusion.159
  1207.8 14.5 fusion.160
  1244.1 15.9 reshape.586
  1260.0 15.9 reshape.585
  1275.9 23.2 maximum_add_fusion.3
  1299.1 106.0 %dynamic_update_slice.28 = f32[128,193,256]{1,0,2:T(8,128)} dynamic-update-slice(f32[128,193,256]{1,0,2:T(8,128)} %get-tuple-element.747, f32[128,97,256]{1,0,2:T(8,128)} %maximum_add_fusion.3, s32[]{:T(128)} %constant.62.clone.1..sunk.3, s32[]{:T(128)S(6)} %select_n.66, s32[]{:T(128)} %constant.62.clone.1..sunk.3) | dynamic-update-slice | bytes 25427972 | tf_op jit(solution)/shard_map/while/body/eval_jaxpr/dynamic_update_slice | solution.py:337
  1450.0 15.1 fusion.159
  1465.0 14.5 fusion.160
  1501.3 15.9 reshape.586
  1517.2 15.9 reshape.585
  1533.1 23.2 maximum_add_fusion.3
  1556.3 106.0 %dynamic_update_slice.28 = f32[128,193,256]{1,0,2:T(8,128)} dynamic-update-slice(f32[128,193,256]{1,0,2:T(8,128)} %get-tuple-element.747, f32[128,97,256]{1,0,2:T(8,128)} %maximum_add_fusion.3, s32[]{:T(128)} %constant.62.clone.1..sunk.3, s32[]{:T(128)S(6)} %select_n.66, s32[]{:T(128)} %constant.62.clone.1..sunk.3) | dynamic-update-slice | bytes 25427972 | tf_op jit(solution)/shard_map/while/body/eval_jaxpr/dynamic_update_slice | solution.py:337
  1674.5 13.7 copy.196
  1697.6 365.9 %fusion.1 = f32[48,896]{1,0:T(8,128)S(1)} fusion(f32[4864,896]{1,0:T(8,128)} %fusion.60), kind=kCustom, calls=%all-reduce-scatter.1 | all-reduce-scatter fusion | flops 5505025 | bytes 17604608
  2090.1 18.2 fusion.56
  2108.4 240.2 %reduce-scatter.7.cloned.1.call-done = f32[128,256]{0,1:T(8,128)} async-done(((f32[16384,256]{0,1:T(8,128)}), f32[128,256]{0,1:T(8,128)}) %reduce-scatter.7.cloned.1.call-update) | async-done | bytes 131088 | tf_op jit(solution)/shard_map/reduce_scatter | solution.py:345
  2369.1 15.9 collective-permute-start.30
  2433.5 414.0 %fusion = f32[8,9728]{1,0:T(8,128)S(1)} fusion(f32[896,9728]{1,0:T(8,128)} %fusion.56), kind=kCustom, calls=%all-reduce-scatter | all-reduce-scatter fusion | flops 9961473 | bytes 35176448
  2872.4 33.3 %all-to-all-start.1 = ((bf16[128,2,448]{2,1,0:T(2,128)(2,1)}), bf16[128,2,448]{2,1,0:T(2,128)(2,1)S(1)}, u32[]{:S(2)}, u32[]{:S(2)}) async-start(bf16[128,2,448]{2,1,0:T(2,128)(2,1)} %reshape.563), calls=%async_computation.1 | async-start | bytes 524288 | tf_op jit(solution)/shard_map/all_to_all | solution.py:395
  2961.7 23.8 all-to-all-start.3
  2985.6 45.5 %concatenate.50 = f32[1318,896]{1,0:T(8,128)} concatenate(f32[22,896]{1,0:T(8,128)} %collective-permute-done.42, f32[48,896]{1,0:T(8,128)} %collective-permute-done.41, f32[48,896]{1,0:T(8,128)} %collective-permute-done.40, f32[48,896]{1,0:T(8,128)} %collective-permute-done.39, f32[48,896]{1,0:T(8,128)} %collective-permute-done.38, f32[48,896]{1,0:T(8,128)S(1)} %copy-done.39, ...), dimensions={0} | concatenate | bytes 9447424
  3034.0 69.0 %concatenate.49 = f32[135,9728]{1,0:T(8,128)} concatenate(f32[7,9728]{1,0:T(8,128)S(1)} %copy-done.31, f32[8,9728]{1,0:T(8,128)} %collective-permute-done.14, f32[8,9728]{1,0:T(8,128)} %collective-permute-done.13, f32[8,9728]{1,0:T(8,128)} %collective-permute-done.12, f32[8,9728]{1,0:T(8,128)} %collective-permute-done.11, f32[8,9728]{1,0:T(8,128)} %collective-permute-done.10, ...), dimensions={0} | concatenate | bytes 10506240
  3105.0 67.3 %all-reduce.8 = f32[2,896]{1,0:T(2,128)S(1)} all-reduce(f32[2,896]{1,0:T(2,128)S(1)} %pad_maximum_fusion.6), channel_id=7, replica_groups=mesh['fsdp'=128] {'fsdp'}, use_global_device_ids=true, to_apply=%region_26.27.clone | all-reduce | flops 1792 | bytes 14336
  3180.4 62.5 %psum.7 = f32[]{:T(128)} all-reduce(f32[]{:T(128)S(6)} %add.289), channel_id=1, replica_groups=mesh['fsdp'=128] {'fsdp'}, use_global_device_ids=true, to_apply=%region_28.29 | all-reduce | flops 1 | bytes 8 | tf_op jit(solution)/shard_map/psum | solution.py:374
  (506 shorter events, 838.0 us)
Async XLA Ops:
  7.2 73.4 %all-gather.16.cloned.1.call-start = ((), (), s32[]{:S(2)}) async-start(), calls=%async_computation.8 | async-start | bytes 2377728 | tf_op jit(solution)/shard_map/all_gather | solution.py:180
  8.6 138.4 %all-gather.18.cloned.1.call-start = ((), (), s32[]{:S(2)}) async-start(), calls=%async_computation.9 | async-start | bytes 1849344 | tf_op jit(solution)/shard_map/all_gather | solution.py:181
  14.8 45.9 %all-to-all-start = ((bf16[128,2,448]{2,1,0:T(2,128)(2,1)}), bf16[128,2,448]{2,1,0:T(2,128)(2,1)S(1)}, u32[]{:S(2)}, u32[]{:S(2)}) async-start(bf16[128,2,448]{2,1,0:T(2,128)(2,1)} %reshape.561), calls=%async_computation | async-start | bytes 524288 | tf_op jit(solution)/shard_map/all_to_all | solution.py:154
  26.3 188.7 %all-gather.12.cloned.1.call-start = ((), (), s32[]{:S(2)}) async-start(), calls=%async_computation.5 | async-start | bytes 4227072 | tf_op jit(solution)/shard_map/all_gather | solution.py:204
  84.6 198.4 %all-gather.14.cloned.1.call-start = ((), (), s32[]{:S(2)}) async-start(), calls=%async_computation.6 | async-start | bytes 4227072 | tf_op jit(solution)/shard_map/all_gather | solution.py:203
  86.2 498.8 %all-gather.22.cloned.1.call-start = ((), (), s32[]{:S(2)}) async-start(), calls=%async_computation.11 | async-start | bytes 9246720 | tf_op jit(solution)/shard_map/all_gather | solution.py:248
  98.0 500.1 %all-gather.20.cloned.1.call-start = ((), (), s32[]{:S(2)}) async-start(), calls=%async_computation.10 | async-start | bytes 20078592 | tf_op jit(solution)/shard_map/all_gather | solution.py:247
  99.7 2248.9 %reduce-scatter.7.cloned.1.call-start = ((), (), s32[]{:S(2)}) async-start(), calls=%async_computation.7 | async-start | bytes 16908288 | tf_op jit(solution)/shard_map/reduce_scatter | solution.py:345
  1688.3 1485.2 %all-reduce.14.cloned.1.call-start = ((), (), s32[]{:S(2)}) async-start(), calls=%async_computation.12 | async-start | bytes 14680064
  2064.1 286.6 %collective-permute-start.41 = (f32[48,896]{1,0:T(8,128)S(1)}, f32[48,896]{1,0:T(8,128)}, u32[]{:S(2)}, u32[]{:S(2)}) collective-permute-start(f32[48,896]{1,0:T(8,128)S(1)} %fusion.1), channel_id=1, source_target_pairs={{0,26},{1,27},{2,28},{3,29},{4,30},{5,31},{6,32},{7,33},{8,34},{9,... | collective-permute-start | bytes 516104
  2066.1 286.0 %collective-permute-start.40 = (f32[48,896]{1,0:T(8,128)S(1)}, f32[48,896]{1,0:T(8,128)}, u32[]{:S(2)}, u32[]{:S(2)}) collective-permute-start(f32[48,896]{1,0:T(8,128)S(1)} %fusion.1), channel_id=1, source_target_pairs={{0,25},{1,26},{2,27},{3,28},{4,29},{5,30},{6,31},{7,32},{8,33},{9,... | collective-permute-start | bytes 516104
  2068.0 285.4 %collective-permute-start.39 = (f32[48,896]{1,0:T(8,128)S(1)}, f32[48,896]{1,0:T(8,128)}, u32[]{:S(2)}, u32[]{:S(2)}) collective-permute-start(f32[48,896]{1,0:T(8,128)S(1)} %fusion.1), channel_id=1, source_target_pairs={{0,24},{1,25},{2,26},{3,27},{4,28},{5,29},{6,30},{7,31},{8,32},{9,... | collective-permute-start | bytes 516104
  2070.0 285.4 %collective-permute-start.38 = (f32[48,896]{1,0:T(8,128)S(1)}, f32[48,896]{1,0:T(8,128)}, u32[]{:S(2)}, u32[]{:S(2)}) collective-permute-start(f32[48,896]{1,0:T(8,128)S(1)} %fusion.1), channel_id=1, source_target_pairs={{0,23},{1,24},{2,25},{3,26},{4,27},{5,28},{6,29},{7,30},{8,31},{9,... | collective-permute-start | bytes 516104
  2074.7 274.8 %collective-permute-start.42 = (f32[22,896]{1,0:T(8,128)}, f32[22,896]{1,0:T(8,128)}, u32[]{:S(2)}, u32[]{:S(2)}) collective-permute-start(f32[22,896]{1,0:T(8,128)} %slice.96), channel_id=1, source_target_pairs={{0,27},{1,28},{2,29},{3,30},{4,31},{5,32},{6,33},{7,34},{8,35},{9,... | collective-permute-start | bytes 236552
  2350.8 16.3 collective-permute-start.36
  2352.1 17.0 collective-permute-start.35
  2353.4 33.5 %collective-permute-start.34 = (f32[48,896]{1,0:T(8,128)S(1)}, f32[48,896]{1,0:T(8,128)}, u32[]{:S(2)}, u32[]{:S(2)}) collective-permute-start(f32[48,896]{1,0:T(8,128)S(1)} %fusion.1), channel_id=1, source_target_pairs={{0,19},{1,20},{2,21},{3,22},{4,23},{5,24},{6,25},{7,26},{8,27},{9,... | collective-permute-start | bytes 516104
  2355.4 34.4 %collective-permute-start.33 = (f32[48,896]{1,0:T(8,128)S(1)}, f32[48,896]{1,0:T(8,128)}, u32[]{:S(2)}, u32[]{:S(2)}) collective-permute-start(f32[48,896]{1,0:T(8,128)S(1)} %fusion.1), channel_id=1, source_target_pairs={{0,18},{1,19},{2,20},{3,21},{4,22},{5,23},{6,24},{7,25},{8,26},{9,... | collective-permute-start | bytes 516104
  2357.4 36.0 %collective-permute-start.32 = (f32[48,896]{1,0:T(8,128)S(1)}, f32[48,896]{1,0:T(8,128)}, u32[]{:S(2)}, u32[]{:S(2)}) collective-permute-start(f32[48,896]{1,0:T(8,128)S(1)} %fusion.1), channel_id=1, source_target_pairs={{0,17},{1,18},{2,19},{3,20},{4,21},{5,22},{6,23},{7,24},{8,25},{9,... | collective-permute-start | bytes 516104
  2367.1 28.2 collective-permute-start.31
  2369.1 30.1 collective-permute-start.30
  2386.9 22.3 collective-permute-start.29
  2389.8 21.1 collective-permute-start.28
  2393.3 28.0 collective-permute-start.27
  2395.3 28.0 collective-permute-start.26
  2399.2 31.4 collective-permute-start.25
  2409.2 438.4 %collective-permute-start.24 = (f32[48,896]{1,0:T(8,128)S(1)}, f32[48,896]{1,0:T(8,128)S(1)}, u32[]{:S(2)}, u32[]{:S(2)}) collective-permute-start(f32[48,896]{1,0:T(8,128)S(1)} %fusion.1), channel_id=1, source_target_pairs={{0,9},{1,10},{2,11},{3,12},{4,13},{5,14},{6,15},{7,16},{8,17},{9,1... | collective-permute-start | bytes 516104
  2410.9 438.0 %collective-permute-start.23 = (f32[48,896]{1,0:T(8,128)S(1)}, f32[48,896]{1,0:T(8,128)}, u32[]{:S(2)}, u32[]{:S(2)}) collective-permute-start(f32[48,896]{1,0:T(8,128)S(1)} %fusion.1), channel_id=1, source_target_pairs={{0,8},{1,9},{2,10},{3,11},{4,12},{5,13},{6,14},{7,15},{8,16},{9,17... | collective-permute-start | bytes 516104
  2421.3 428.9 %collective-permute-start.22 = (f32[48,896]{1,0:T(8,128)S(1)}, f32[48,896]{1,0:T(8,128)}, u32[]{:S(2)}, u32[]{:S(2)}) collective-permute-start(f32[48,896]{1,0:T(8,128)S(1)} %fusion.1), channel_id=1, source_target_pairs={{0,7},{1,8},{2,9},{3,10},{4,11},{5,12},{6,13},{7,14},{8,15},{9,16}... | collective-permute-start | bytes 516104
  2423.3 428.2 %collective-permute-start.21 = (f32[48,896]{1,0:T(8,128)S(1)}, f32[48,896]{1,0:T(8,128)}, u32[]{:S(2)}, u32[]{:S(2)}) collective-permute-start(f32[48,896]{1,0:T(8,128)S(1)} %fusion.1), channel_id=1, source_target_pairs={{0,6},{1,7},{2,8},{3,9},{4,10},{5,11},{6,12},{7,13},{8,14},{9,15},... | collective-permute-start | bytes 516104
  2430.6 422.3 %collective-permute-start.20 = (f32[48,896]{1,0:T(8,128)S(1)}, f32[48,896]{1,0:T(8,128)}, u32[]{:S(2)}, u32[]{:S(2)}) collective-permute-start(f32[48,896]{1,0:T(8,128)S(1)} %fusion.1), channel_id=1, source_target_pairs={{0,5},{1,6},{2,7},{3,8},{4,9},{5,10},{6,11},{7,12},{8,13},{9,14},{... | collective-permute-start | bytes 516104
  2854.8 50.9 %collective-permute-start.14 = (f32[8,9728]{1,0:T(8,128)S(1)}, f32[8,9728]{1,0:T(8,128)}, u32[]{:S(2)}, u32[]{:S(2)}) collective-permute-start(f32[8,9728]{1,0:T(8,128)S(1)} %fusion), channel_id=1, source_target_pairs={{0,15},{1,16},{2,17},{3,18},{4,19},{5,20},{6,21},{7,22},{8,23},{9,... | collective-permute-start | bytes 933896
  2856.9 53.3 %collective-permute-start.13 = (f32[8,9728]{1,0:T(8,128)S(1)}, f32[8,9728]{1,0:T(8,128)}, u32[]{:S(2)}, u32[]{:S(2)}) collective-permute-start(f32[8,9728]{1,0:T(8,128)S(1)} %fusion), channel_id=1, source_target_pairs={{0,14},{1,15},{2,16},{3,17},{4,18},{5,19},{6,20},{7,21},{8,22},{9,... | collective-permute-start | bytes 933896
  2858.9 56.1 %collective-permute-start.12 = (f32[8,9728]{1,0:T(8,128)S(1)}, f32[8,9728]{1,0:T(8,128)}, u32[]{:S(2)}, u32[]{:S(2)}) collective-permute-start(f32[8,9728]{1,0:T(8,128)S(1)} %fusion), channel_id=1, source_target_pairs={{0,13},{1,14},{2,15},{3,16},{4,17},{5,18},{6,19},{7,20},{8,21},{9,... | collective-permute-start | bytes 933896
  2860.9 57.1 %collective-permute-start.11 = (f32[8,9728]{1,0:T(8,128)S(1)}, f32[8,9728]{1,0:T(8,128)}, u32[]{:S(2)}, u32[]{:S(2)}) collective-permute-start(f32[8,9728]{1,0:T(8,128)S(1)} %fusion), channel_id=1, source_target_pairs={{0,12},{1,13},{2,14},{3,15},{4,16},{5,17},{6,18},{7,19},{8,20},{9,... | collective-permute-start | bytes 933896
  2863.7 55.9 %collective-permute-start.10 = (f32[8,9728]{1,0:T(8,128)S(1)}, f32[8,9728]{1,0:T(8,128)}, u32[]{:S(2)}, u32[]{:S(2)}) collective-permute-start(f32[8,9728]{1,0:T(8,128)S(1)} %fusion), channel_id=1, source_target_pairs={{0,11},{1,12},{2,13},{3,14},{4,15},{5,16},{6,17},{7,18},{8,19},{9,... | collective-permute-start | bytes 933896
  2872.4 89.3 %all-to-all-start.1 = ((bf16[128,2,448]{2,1,0:T(2,128)(2,1)}), bf16[128,2,448]{2,1,0:T(2,128)(2,1)S(1)}, u32[]{:S(2)}, u32[]{:S(2)}) async-start(bf16[128,2,448]{2,1,0:T(2,128)(2,1)} %reshape.563), calls=%async_computation.1 | async-start | bytes 524288 | tf_op jit(solution)/shard_map/all_to_all | solution.py:395
  2905.8 20.8 collective-permute-start.9
  2910.2 21.7 collective-permute-start.8
  2915.0 32.1 collective-permute-start.7
  2918.1 37.6 %collective-permute-start.6 = (f32[8,9728]{1,0:T(8,128)S(1)}, f32[8,9728]{1,0:T(8,128)S(1)}, u32[]{:S(2)}, u32[]{:S(2)}) collective-permute-start(f32[8,9728]{1,0:T(8,128)S(1)} %fusion), channel_id=1, source_target_pairs={{0,7},{1,8},{2,9},{3,10},{4,11},{5,12},{6,13},{7,14},{8,15},{9,16}... | collective-permute-start | bytes 933896
  2919.6 38.1 %collective-permute-start.5 = (f32[8,9728]{1,0:T(8,128)S(1)}, f32[8,9728]{1,0:T(8,128)S(1)}, u32[]{:S(2)}, u32[]{:S(2)}) collective-permute-start(f32[8,9728]{1,0:T(8,128)S(1)} %fusion), channel_id=1, source_target_pairs={{0,6},{1,7},{2,8},{3,9},{4,10},{5,11},{6,12},{7,13},{8,14},{9,15},... | collective-permute-start | bytes 933896
  2926.6 107.3 %collective-permute-start.4 = (f32[8,9728]{1,0:T(8,128)S(1)}, f32[8,9728]{1,0:T(8,128)}, u32[]{:S(2)}, u32[]{:S(2)}) collective-permute-start(f32[8,9728]{1,0:T(8,128)S(1)} %fusion), channel_id=1, source_target_pairs={{0,5},{1,6},{2,7},{3,8},{4,9},{5,10},{6,11},{7,12},{8,13},{9,14},{... | collective-permute-start | bytes 933896
  2931.9 102.1 %collective-permute-start.3 = (f32[8,9728]{1,0:T(8,128)S(1)}, f32[8,9728]{1,0:T(8,128)}, u32[]{:S(2)}, u32[]{:S(2)}) collective-permute-start(f32[8,9728]{1,0:T(8,128)S(1)} %fusion), channel_id=1, source_target_pairs={{0,4},{1,5},{2,6},{3,7},{4,8},{5,9},{6,10},{7,11},{8,12},{9,13},{1... | collective-permute-start | bytes 933896
  2947.0 86.9 %collective-permute-start.2 = (f32[8,9728]{1,0:T(8,128)S(1)}, f32[8,9728]{1,0:T(8,128)}, u32[]{:S(2)}, u32[]{:S(2)}) collective-permute-start(f32[8,9728]{1,0:T(8,128)S(1)} %fusion), channel_id=1, source_target_pairs={{0,3},{1,4},{2,5},{3,6},{4,7},{5,8},{6,9},{7,10},{8,11},{9,12},{10... | collective-permute-start | bytes 933896
  2955.7 78.3 %collective-permute-start.1 = (f32[8,9728]{1,0:T(8,128)S(1)}, f32[8,9728]{1,0:T(8,128)}, u32[]{:S(2)}, u32[]{:S(2)}) collective-permute-start(f32[8,9728]{1,0:T(8,128)S(1)} %fusion), channel_id=1, source_target_pairs={{0,2},{1,3},{2,4},{3,5},{4,6},{5,7},{6,8},{7,9},{8,10},{9,11},{10,... | collective-permute-start | bytes 933896
  2957.7 76.3 %collective-permute-start = (f32[8,9728]{1,0:T(8,128)S(1)}, f32[8,9728]{1,0:T(8,128)}, u32[]{:S(2)}, u32[]{:S(2)}) collective-permute-start(f32[8,9728]{1,0:T(8,128)S(1)} %fusion), channel_id=1, source_target_pairs={{0,1},{1,2},{2,3},{3,4},{4,5},{5,6},{6,7},{7,8},{8,9},{9,10},{10,1... | collective-permute-start | bytes 933896
  2961.7 211.2 %all-to-all-start.3 = ((bf16[128,2,448]{2,1,0:T(2,128)(2,1)}), bf16[128,2,448]{2,1,0:T(2,128)(2,1)S(1)}, u32[]{:S(2)}, u32[]{:S(2)}) async-start(bf16[128,2,448]{2,1,0:T(2,128)(2,1)} %reshape.567), calls=%async_computation.4 | async-start | bytes 524288 | tf_op jit(solution)/shard_map/all_to_all | solution.py:402
  (78 other events, 5168.1 us)
Sparse Core Ops, SparseCore 0:
  11.6 68.9 all-gather.15
  84.0 62.9 all-gather.17
  150.7 64.2 all-gather.11
  218.6 64.3 all-gather.13
  286.5 68.0 all-gather.21
  358.0 82.8 all-gather.19
  1688.4 660.1 reduce-scatter.6
  2409.3 195.8 all-reduce.13
where the time goes:
time: 3290 us; the launch traced here: 3260 us
  local copies, waits for them, and re-layouts  1030 us (31%)
  blocking collectives  942 us (29%)
  waiting for transfers between devices  445 us (14%)
  matrix products  362 us (11%)
  other arithmetic  234 us (7%)
  starting transfers between devices  220 us (7%)
    unnamed x3, blocking collectives  847 us
    dynamic_update_slice x4, local copies, waits for them, and re-layouts, back_step(): lax.dynamic_update_slice_in_dim(pad_grads, current + both_parts, first_ro...  398 us
    reduce_scatter x1, waiting for transfers between devices, body(): lax.psum_scatter(pad_grads[:, reach_rows:, :].reshape(devices * local_row...  240 us
    unnamed x154, local copies, waits for them, and re-layouts  182 us
    unnamed x44, starting transfers between devices  145 us
    dot_general x8, matrix products, window_scores(): jnp.einsum('qkgd,skd->kgqs', block_query, key_window, preferred_element_t...  115 us
    add x4, other arithmetic, back_step(): current + both_parts  92.7 us
  transfers between devices with their start and end apart: 55, of which 8 were waited for; matrix products, arithmetic and copies ran while one was open for 40% of the time, Pallas kernels for 0%

commit v1 on v0

v1 whole, which is shorter than its diff:
```python
import jax
import jax.numpy as jnp
import numpy as np
from jax import lax
from jax.experimental import pallas as pl
from jax.experimental.pallas import tpu as pltpu
from jax.sharding import Mesh
from jax.sharding import PartitionSpec as P

D = 896
FF = 4864
HEADS = 14
KV_HEADS = 2
HEAD_DIM = 64
DOCS = 6
STEP = 10

norm_eps = 1e-05
rope_base = 130000.0
beta_first = 0.9
beta_second = 0.95
adam_eps = 1e-08
decay_rate = 0.1
matrix_rate = 4.0
gain_rate = 1.5
masked_score = -1e30

ALL = ("y", "z", "x", "c")
RING = 4
DEVICES = 128
CHIPS = 64
LOCAL = 128
CHIP = 2 * LOCAL
GROUP = HEADS // KV_HEADS
HALF_Q = GROUP * HEAD_DIM
RANKS = 8
SLICE = FF // RANKS
DOWN_ROWS = FF // DEVICES
DOWN_PAD = 48
SPAN = 16
BLOCKS = LOCAL // SPAN
TILE = SPAN * DEVICES
HALF = SPAN // 2
HALF_TILE = TILE // 2
HALF_ROWS = GROUP * SPAN
QROWS = 2 * HALF_ROWS
QPAD = 256
WIDE = 8 * DEVICES
IN_COLS, OUT_COLS = 640, 512
ATT_COLS = IN_COLS + OUT_COLS
HEADS_6 = 6 * HEAD_DIM
LATE = 2 * HEADS_6
LAST = LATE + 256
GAIN_AT = LAST + HEAD_DIM
HID = 640
MESH = pl.DeviceIdType.MESH
VM, ANY = pltpu.VMEM, pl.ANY
bf16 = jnp.bfloat16
f32 = jnp.float32


def widen_matrix(turned=False):
    place = np.arange(WIDE)
    picks = np.zeros((D, WIDE), np.float32)
    kept = place % 8 < 7
    picks[(7 * (place // 8) + place % 8)[kept], place[kept]] = 1
    return jnp.asarray(picks.T if turned else picks, bf16)


def pack_matrix():
    unit = np.arange(SLICE)
    picks = np.zeros((HID, 16 * DOWN_PAD), np.float32)
    picks[unit, DOWN_PAD * (unit // DOWN_ROWS) + unit % DOWN_ROWS] = 1
    return jnp.asarray(picks, bf16)


def turn_matrix():
    place = np.arange(DEVICES)
    picks = np.zeros((DEVICES, DEVICES), np.float32)
    picks[place % RANKS * 16 + place // RANKS, place] = 1
    return jnp.asarray(picks, bf16)


def order_matrix():
    place = np.arange(CHIP)
    picks = np.zeros((CHIP, CHIP), np.float32)
    picks[(place % LOCAL // 8 * 2 + place // LOCAL) * 8 + place % 8, place] = 1
    return jnp.asarray(picks, bf16)


def swap_matrix():
    place = np.arange(DEVICES)
    picks = np.zeros((DEVICES, DEVICES), np.float32)
    picks[place // 8 % RING * 32 + place // 32 * 8 + place % 8, place] = 1
    return jnp.asarray(picks, bf16)


def step_along(axis, delta):
    size = 2 if axis == "c" else RING
    return {axis: lax.rem(lax.axis_index(axis) + (delta + size), size)}


def shifted(axis, delta):
    return lax.rem(lax.axis_index(axis) + (delta + RING), RING)


def axis_peers(axes):
    peers = []
    for axis in axes:
        peers += [step_along(axis, delta) for delta in ((1,) if axis == "c" else (1, 2, 3))]
    return peers


def line_peers():
    x, c = lax.axis_index("x"), lax.axis_index("c")
    return [
        {"x": lax.rem(x + dx, RING), "c": lax.rem(c + dc, 2)}
        for dx in range(RING)
        for dc in range(2)
        if dx or dc
    ]


def device_number():
    y, z, x, c = (lax.axis_index(axis) for axis in ALL)
    return ((y * RING + z) * RING + x) * 2 + c


def place(index):
    return {
        "y": index // 32,
        "z": lax.rem(index // 8, 4),
        "x": lax.rem(index // 2, 4),
        "c": lax.rem(index, 2),
    }


def greet(peers, target=None, source=None):
    barrier = pltpu.get_barrier_semaphore()
    for peer in peers:
        pl.semaphore_signal(barrier, inc=1, device_id=peer, device_id_type=MESH)
    if target is None:
        pl.semaphore_wait(barrier, len(peers))
        return
    me = device_number()

    @pl.when(target != me)
    def _():
        pl.semaphore_signal(barrier, inc=1, device_id=place(source), device_id_type=MESH)
        pl.semaphore_wait(barrier, len(peers) + 1)

    @pl.when(target == me)
    def _():
        pl.semaphore_wait(barrier, len(peers))


class Sems:
    def __init__(self, send, recv):
        self.send, self.recv, self.used = send, recv, 0

    def copy(self, src, dst, device):
        at = self.used
        self.used += 1
        return pltpu.make_async_remote_copy(
            src_ref=src,
            dst_ref=dst,
            send_sem=self.send.at[at],
            recv_sem=self.recv.at[at],
            device_id=device,
            device_id_type=MESH,
        )

    def local(self, src, dst):
        at = self.used
        self.used += 1
        return pltpu.make_async_copy(src, dst, self.send.at[at])

    def fetch(self, src, dst):
        copy = self.local(src, dst)
        copy.start()
        return copy


def together(*steps):
    running = list(steps)
    while running:
        for step in list(running):
            try:
                next(step)
            except StopIteration:
                running.remove(step)


def gather_direct(sems, axis, part):
    me = shifted(axis, 0)
    copies = [sems.copy(part(me), part(me), step_along(axis, d)) for d in (1, 3, 2)]
    for copy in copies:
        copy.start()
    yield
    for copy in copies:
        copy.wait()


def gather_ring(sems, axis, part, half):
    me, left, right = shifted(axis, 0), shifted(axis, -1), shifted(axis, 1)
    to_right = sems.copy(part(me), part(me), step_along(axis, 1))
    to_left = sems.copy(part(me), part(me), step_along(axis, -1))
    to_right.start()
    to_left.start()
    yield
    to_right.wait_recv()
    on_right = sems.copy(half(left, 0), half(left, 0), step_along(axis, 1))
    on_right.start()
    to_left.wait_recv()
    on_left = sems.copy(half(right, 1), half(right, 1), step_along(axis, -1))
    on_left.start()
    yield
    on_right.wait_recv()
    on_left.wait_recv()
    for copy in (to_right, to_left, on_right, on_left):
        copy.wait_send()


def chip_gather(sems, order, buf):
    for number, axis in enumerate(order):
        own = tuple(lax.axis_index(a) for a in reversed(order[number + 1 :]))

        def part(i, own=own):
            return buf.at[(*own, i)]

        if number < len(order) - 1:
            yield from gather_direct(sems, axis, part)
        else:
            yield from gather_ring(sems, axis, part, lambda i, h: buf.at[i, pl.ds(2 * h, 2)])


def own_place(axes):
    return tuple(lax.axis_index(axis) for axis in axes)


def natural(axes):
    return [
        tuple({"y": y, "z": z, "x": x}[axis] for axis in axes)
        for y in range(RING)
        for z in range(RING)
        for x in range(RING)
    ]


def in_turn(phases):
    for phase in phases:
        phase()
        yield


def gather_line(sems, all_ref):
    x, c = lax.axis_index("x"), lax.axis_index("c")
    sibling, right, left = step_along("c", 1), step_along("x", 1), step_along("x", -1)
    at_left, at_right, at_far = shifted("x", -1), shifted("x", 1), shifted("x", 2)
    top, bottom = pl.ds(0, LOCAL // 2), pl.ds(LOCAL // 2, LOCAL // 2)

    def same(ref, device):
        return sems.copy(ref, ref, device)

    mine = all_ref.at[x, c]
    to_right, to_left, to_pair = same(mine, right), same(mine, left), same(mine, sibling)
    on_right = same(all_ref.at[at_left, c, top], right)
    on_left = same(all_ref.at[at_right, c, bottom], left)
    pair_left = same(all_ref.at[at_left, c], sibling)
    pair_right = same(all_ref.at[at_right, c], sibling)
    pair_far = same(all_ref.at[at_far, c], sibling)

    def start():
        to_right.start()
        to_left.start()
        to_pair.start()

    def relay():
        to_right.wait_recv()
        on_right.start()
        pair_left.start()
        to_left.wait_recv()
        on_left.start()
        pair_right.start()
        pair_left.wait_recv()

    def relay_far():
        on_right.wait_recv()
        on_left.wait_recv()
        pair_far.start()

    def close():
        for copy in (to_right, to_left, to_pair, on_right, on_left, pair_left, pair_right, pair_far):
            copy.wait_send()

    return start, to_pair.wait_recv, relay, pair_right.wait_recv, relay_far, pair_far.wait_recv, close


def add_into(out, *terms):
    total = terms[0][...].astype(f32)
    for term in terms[1:]:
        total = total + term[...].astype(f32)
    out[...] = total.astype(out.dtype)


def half_of(ref, h):
    return ref.at[pl.ds(2 * h, 2)]


def reduce_ring(sems, axis, part, bufs, out):
    first, next_right, next_left, last_left, last_right = bufs
    me, left, right, far = (shifted(axis, d) for d in (0, -1, 1, 2))
    one = sems.copy(half_of(part(far), 0), half_of(first, 0), step_along(axis, 1))
    two = sems.copy(half_of(part(far), 1), half_of(first, 1), step_along(axis, -1))
    one.start()
    two.start()
    half_of(next_right, 1)[...] = half_of(part(right), 1)[...]
    half_of(next_left, 0)[...] = half_of(part(left), 0)[...]
    yield
    one.wait_recv()
    add_into(half_of(next_right, 0), half_of(part(right), 0), half_of(first, 0))
    three = sems.copy(next_right, last_left, step_along(axis, 1))
    three.start()
    two.wait_recv()
    add_into(half_of(next_left, 1), half_of(part(left), 1), half_of(first, 1))
    four = sems.copy(next_left, last_right, step_along(axis, -1))
    four.start()
    yield
    three.wait_recv()
    four.wait_recv()
    add_into(out, part(me), last_left, last_right)
    for copy in (one, two, three, four):
        copy.wait_send()


def reduce_direct(sems, axis, part, inbox, out):
    copies = [
        sems.copy(part(shifted(axis, d)), inbox.at[d - 1], step_along(axis, d)) for d in (1, 3, 2)
    ]
    for copy in copies:
        copy.start()
    yield
    for copy in copies:
        copy.wait_recv()
    add_into(out, part(shifted(axis, 0)), *(inbox.at[d] for d in range(3)))
    for copy in copies:
        copy.wait_send()


def chip_reduce(sems, order, source, scratch):
    scratch = list(scratch)
    if len(scratch) == 2 * len(order):
        total = None
    else:
        bufs, total = scratch[:5], scratch[5]
        yield from reduce_ring(sems, order[0], source, bufs, total)
        del scratch[:6]
    for axis in order[0 if total is None else 1 :]:
        inbox, out = scratch[:2]
        del scratch[:2]
        part = source if total is None else (lambda i, t=total: t.at[i])
        yield from reduce_direct(sems, axis, part, inbox, out)
        total = out


def reduce_scratch(order, tail, ring=True):
    count = len(order)
    lead = (RING,) * (count - 1)
    scratch = [VM(lead + tail, bf16) for _ in range(6)] if ring else []
    for number in range(1 if ring else 0, count):
        shape = (RING,) * (count - 1 - number) + tail
        scratch.append(VM((3,) + shape, bf16))
        scratch.append(VM(shape, f32 if number == count - 1 else bf16))
    return scratch


def remote_call(kernel, outs, ins, scratch, copies, collective, *args):
    return pl.pallas_call(
        kernel,
        out_shape=[jax.ShapeDtypeStruct(shape, dtype) for shape, dtype, _ in outs],
        in_specs=[pl.BlockSpec(memory_space=space) for space in ins],
        out_specs=[pl.BlockSpec(memory_space=space) for _, _, space in outs],
        scratch_shapes=list(scratch)
        + [pltpu.SemaphoreType.DMA((copies,)), pltpu.SemaphoreType.DMA((copies,))],
        compiler_params=pltpu.CompilerParams(
            collective_id=collective, has_side_effects=True, vmem_limit_bytes=60 << 20
        ),
    )(*args)


def mm(left, right, dims):
    return lax.dot_general(left, right, ((dims[0], dims[1]), ((), ())), preferred_element_type=f32)


NN, NT, TN = ((1,), (0,)), ((1,), (1,)), ((0,), (0,))


def inverse_norm(values):
    return lax.rsqrt(jnp.sum(values * values, axis=-1, keepdims=True) / D + norm_eps)


def norm_back(values, scale, delta, gain):
    turned = delta * gain
    along = jnp.sum(turned * values, axis=-1, keepdims=True) / D
    return scale * turned - values * (scale * scale * scale) * along


def roll_halves(values):
    lane = lax.broadcasted_iota(jnp.int32, values.shape, 1)
    low = (lane & (HEAD_DIM - 1)) < HEAD_DIM // 2
    return jnp.where(
        low, pltpu.roll(values, 2 * HEAD_DIM - HEAD_DIM // 2, 1), pltpu.roll(values, HEAD_DIM // 2, 1)
    )


def pick(matrix, rows, dims=NN):
    return mm(matrix, rows, dims).astype(bf16)


def deal_line(sems, rows, out, turn_ref, held):
    x, c = lax.axis_index("x"), lax.axis_index("c")
    width = rows.shape[-1]
    held[...] = pick(turn_ref[...], rows).reshape(RING, 2, 16, width)
    copies = [sems.copy(held.at[peer["x"], peer["c"]], out.at[x, c], peer) for peer in line_peers()]
    for copy in copies:
        copy.start()
    out[x, c] = held[x, c]
    yield
    for copy in copies:
        copy.wait()


def deal_plane(sems, rows_ref, out, turn_ref, swap_ref, given, taken):
    width = out.shape[-1]
    rows = pick(turn_ref[...], rows_ref[...].reshape(DEVICES, width), TN)
    for number, axis in enumerate("yz"):
        at = lax.axis_index(axis)
        given[number] = rows.reshape(RING, 32, width)
        copies = [
            sems.copy(
                given.at[number, shifted(axis, d)], taken.at[number, at], step_along(axis, d)
            )
            for d in (1, 3, 2)
        ]
        for copy in copies:
            copy.start()
        taken[number, at] = given[number, at]
        yield
        for copy in copies:
            copy.wait()
        rows = pick(swap_ref[...], taken[number].reshape(DEVICES, width))
    out[...] = rows


def eight(rows):
    return jnp.concatenate([rows, jnp.zeros((1, rows.shape[1]), f32)], axis=0)


def spread_kernel(
    tokens_ref,
    cotangent_ref,
    in_ref,
    out_ref,
    gains_ref,
    gate_ref,
    down_ref,
    turn_ref,
    pair_ref,
    line_ref,
    here_ref,
    x_line,
    up_line,
    att,
    gate,
    down,
    att_in,
    gate_in,
    x_held,
    up_held,
    send,
    recv,
):
    x, c = lax.axis_index("x"), lax.axis_index("c")
    me = device_number()
    target = lax.rem(me, 16) * 8 + me // 16
    source = lax.rem(me, 8) * 16 + me // 8
    line = line_peers()
    in_weight, out_weight = eight(in_ref[...]), eight(out_ref[...])
    none = jnp.zeros((8, HEAD_DIM), f32)
    gains = jnp.concatenate([gains_ref[...], jnp.zeros((2, 121), f32)], axis=1)
    before, after = jnp.zeros((HEAD_DIM, 128), f32), jnp.zeros((HEAD_DIM - 2, 128), f32)
    gains = jnp.concatenate([before, gains, after], axis=0).T[:8]
    for h in range(KV_HEADS):
        k_at, v_at = D + HEAD_DIM * h, D + HEAD_DIM * (KV_HEADS + h)
        first, six, last = HALF_Q * h, HALF_Q * h + HEADS_6, HALF_Q * (h + 1)
        att[h] = jnp.concatenate(
            [
                in_weight[:, first:six],
                out_weight[:, first:six],
                in_weight[:, six:last],
                in_weight[:, k_at : k_at + HEAD_DIM],
                in_weight[:, v_at : v_at + HEAD_DIM],
                none,
                out_weight[:, six:last],
                none,
            ],
            axis=1,
        )
        att[h, :, pl.ds(LAST, 128)] += gains
    gate_weight = eight(gate_ref[...])
    none = jnp.zeros((8, HID - SLICE), f32)
    for rank in range(RANKS):
        at = SLICE * rank
        piece = [
            jnp.concatenate([gate_weight[:, at : at + SLICE], none], axis=1),
            jnp.concatenate([gate_weight[:, FF + at : FF + at + SLICE], none], axis=1),
        ]
        gate[rank // 2, rank % 2] = jnp.concatenate(piece, axis=0).astype(bf16)
    down[...] = jnp.concatenate(
        [down_ref[...], jnp.zeros((DOWN_PAD - DOWN_ROWS, D), f32)], axis=0
    ).astype(bf16)
    greet(line, target, source)
    sems = Sems(send, recv)
    swap = sems.copy(att.at[1 - c], att_in, step_along("c", 1))
    swap.start()
    deals = [
        deal_line(sems, tokens_ref[...], x_line, turn_ref, x_held),
        deal_line(sems, cotangent_ref[...], up_line, turn_ref, up_held),
    ]
    next(deals[0])
    shares = [sems.copy(gate.at[peer["x"], peer["c"]], gate_in.at[x, c], peer) for peer in line]
    for copy in shares:
        copy.start()
    move = sems.copy(down, here_ref, place(target))
    stay = sems.local(down, here_ref)

    @pl.when(target != me)
    def _():
        move.start()

    @pl.when(target == me)
    def _():
        stay.start()

    next(deals[1])
    gate_in[x, c] = gate[x, c]
    swap.wait()
    own, other = att[c], att_in[...]
    first = jnp.where(c == 0, own, other)
    second = jnp.where(c == 0, other, own)
    pair_ref[...] = jnp.concatenate([first, second], axis=0).astype(bf16)
    for copy in shares:
        copy.wait()
    for i in range(RING):
        one, two = gate_in[i, 0].astype(f32), gate_in[i, 1].astype(f32)
        left = jnp.concatenate([one[:8], two[:8]], axis=0)
        right = jnp.concatenate([one[8:], two[8:]], axis=0)
        line_ref[i] = jnp.concatenate([left, right], axis=1).astype(bf16)
    together(*deals)

    @pl.when(target != me)
    def _():
        move.wait()

    @pl.when(target == me)
    def _():
        stay.wait()


def spread(*args):
    rows = (RING, 2, 16, D)
    return remote_call(
        spread_kernel,
        [
            ((16, ATT_COLS), bf16, VM),
            ((RING, 16, 2 * HID), bf16, VM),
            ((DOWN_PAD, D), bf16, VM),
            (rows, bf16, VM),
            (rows, bf16, VM),
        ],
        [VM] * 8,
        [
            VM((2, 8, ATT_COLS), f32),
            VM((RING, 2, 16, HID), bf16),
            VM((DOWN_PAD, D), bf16),
            VM((8, ATT_COLS), f32),
            VM((RING, 2, 16, HID), bf16),
            VM(rows, bf16),
            VM(rows, bf16),
        ],
        32,
        0,
        *args,
    )


KEY_SPLITS = (("xyz", 0, 96), ("zxy", 96, 96), ("yzx", 192, 64))
ROW_SPLITS = (("yzx", 0, 96), ("zxy", 96, 96), ("xyz", 192, 64))
IN_SPLITS = (("xyz", 0, 256), ("yzx", LATE, 256), ("zxy", 256, 128), ("zxy", LAST, 128))
OUT_SPLITS = (("xyz", HEADS_6, 128), ("yzx", HEADS_6 + 128, 128), ("zxy", HEADS_6 + 256, 128))
EARLY_SPLITS = (("xyz", 0, 256), ("yzx", 256, 256), ("zxy", 512, 256))
LATE_SPLITS = (("xyz", LATE, 128), ("yzx", LATE + 128, 128), ("zxy", LAST, 128))


def project_kernel(
    x_line,
    up_in,
    pair_ref,
    turn_ref,
    swap_ref,
    wide_ref,
    order_ref,
    cos_ref,
    sin_ref,
    q_ref,
    normed_ref,
    x_wide_ref,
    gains_ref,
    att_ref,
    kv_first,
    kv_second,
    kv_third,
    up_line,
    x_both,
    up_own,
    wide,
    x_given,
    x_taken,
    up_given,
    up_taken,
    *rest,
):
    cut, (send, recv) = rest[:-2], rest[-2:]
    c = lax.axis_index("c")
    splits = IN_SPLITS + OUT_SPLITS
    for (order, first, lanes), buf in zip(splits, cut):
        buf[own_place(reversed(order))] = pair_ref[:, pl.ds(first, lanes)]
    sems = Sems(send, recv)
    wide_here = sems.fetch(wide_ref, wide)
    greet(axis_peers("yzxc"))

    def settle_columns(number):
        order, first, lanes = splits[number]
        for chip, spot in enumerate(natural(order[::-1])):
            att_ref[chip, :, pl.ds(first, lanes)] = cut[number][spot]

    def advance(*steps):
        for step in steps:
            next(step, None)

    gathers = [chip_gather(sems, split[0], buf) for split, buf in zip(splits, cut)]
    weights, others = gathers[: len(IN_SPLITS)], gathers[len(IN_SPLITS) :]
    deal_x = deal_plane(sems, x_line, x_both.at[c], turn_ref, swap_ref, x_given, x_taken)
    deal_up = deal_plane(sems, up_in, up_own, turn_ref, swap_ref, up_given, up_taken)
    advance(deal_x, *weights)
    advance(deal_x, *weights)
    advance(deal_x)
    swap = sems.copy(x_both.at[c], x_both.at[c], step_along("c", 1))
    swap.start()
    advance(*weights)
    advance(*others)
    advance(deal_up)
    swap.wait()
    wide_here.wait()
    x_wide = mm(x_both[...].reshape(CHIP, D), wide[...], NN)
    x_wide_ref[...] = x_wide.astype(bf16).reshape(2, LOCAL, WIDE)
    scaled = x_wide * inverse_norm(x_wide)
    advance(*weights)
    advance(*others)
    advance(deal_up)
    together(*weights)
    advance(deal_up)
    up_line[own_place("xc")] = up_own[...]
    advance(*others)
    for number in range(len(IN_SPLITS)):
        settle_columns(number)

    gains = att_ref[:, :, pl.ds(LAST, 128)].reshape(WIDE, 128).astype(f32).T
    gains_ref[...] = gains[GAIN_AT - LAST : GAIN_AT - LAST + 8]
    normed = (scaled * gains_ref[0:1]).astype(bf16)
    normed_ref[...] = normed
    joined = jnp.concatenate(
        [
            mm(normed, att_ref[:, :, pl.ds(0, HEADS_6)].reshape(WIDE, HEADS_6), NN),
            mm(normed, att_ref[:, :, pl.ds(LATE, 256)].reshape(WIDE, 256), NN),
        ],
        axis=1,
    )
    cosine, sine = cos_ref[...], sin_ref[...]
    turned = []
    for tile in range(4):
        values = joined[:, 128 * tile : 128 * (tile + 1)]
        turned.append((values * cosine + roll_halves(values) * sine).astype(bf16))
    queries = jnp.concatenate(turned, axis=1)
    q_ref[...] = (queries * jnp.asarray(HEAD_DIM ** (-0.5), bf16)).reshape(2, LOCAL, OUT_COLS)
    keys_values = jnp.concatenate(
        [turned[3][:, HEAD_DIM:], joined[:, OUT_COLS : OUT_COLS + HEAD_DIM].astype(bf16)], axis=1
    )
    keys_values = pick(order_ref[...], keys_values)
    kvs = (kv_first, kv_second, kv_third)
    for (order, first, count), kv in zip(KEY_SPLITS, kvs):
        kv[own_place(reversed(order))] = keys_values[first : first + count]
    together(
        *(chip_gather(sems, split[0], kv) for split, kv in zip(KEY_SPLITS, kvs)),
        *others,
        in_turn(gather_line(sems, up_line)),
    )
    for number in range(len(IN_SPLITS), len(splits)):
        settle_columns(number)


def project(*args):
    return remote_call(
        project_kernel,
        [
            ((2, LOCAL, OUT_COLS), bf16, VM),
            ((CHIP, WIDE), bf16, VM),
            ((2, LOCAL, WIDE), bf16, VM),
            ((8, WIDE), f32, VM),
            ((CHIPS, 16, ATT_COLS), bf16, VM),
            *(
                ((RING, RING, RING, count, 2 * HEAD_DIM), bf16, VM)
                for _, _, count in KEY_SPLITS
            ),
            ((RING, 2, LOCAL, D), bf16, VM),
        ],
        [VM] * 5 + [ANY] + [VM] * 3,
        [
            VM((2, LOCAL, D), bf16),
            VM((LOCAL, D), bf16),
            VM((D, WIDE), bf16),
        ]
        + [VM((2, RING, 32, D), bf16)] * 4
        + [VM((RING, RING, RING, 16, lanes), bf16) for _, _, lanes in IN_SPLITS + OUT_SPLITS],
        128,
        1,
        *args,
    )


def begins(starts_ref, position):
    begin = jnp.zeros_like(position)
    for number in range(DOCS):
        start = starts_ref[number]
        begin = jnp.maximum(begin, jnp.where(position >= start, start, 0))
    return begin


def query_places(block, chip_ref, shape, axis):
    index = lax.broadcasted_iota(jnp.int32, shape, axis)
    row = block * SPAN + ((index >> 4) & 1) * HALF + (index & (HALF - 1))
    return row * DEVICES + chip_ref[0] + ((index >> 3) & 1)


def key_places(shape, axis):
    index = lax.broadcasted_iota(jnp.int32, shape, axis)
    return (index & (HALF - 1)) * DEVICES + (index >> 4) * 2 + ((index >> 3) & 1)


def first_place(tile, piece):
    return tile * TILE + piece // 2 * HALF_TILE + piece % 2 * (PIECE // SPAN * 2)


def tile_range(block, starts_ref, chip_ref):
    first = block * TILE + chip_ref[0]
    last = first + (SPAN - 1) * DEVICES + 1
    low = begins(starts_ref, first) // HALF_TILE
    full = (begins(starts_ref, last) + (TILE - 1)) // TILE
    return low, jnp.minimum(full, block)


def over_tiles(block, starts_ref, chip_ref, step):
    low, full = tile_range(block, starts_ref, chip_ref)
    every, upper = range(PIECES), range(PIECES // 2, PIECES)

    @pl.when(((low & 1) == 1) & (low // 2 < block))
    def _():
        step(low // 2, True, upper, False)

    @pl.loop((low + 1) // 2, full)
    def _(tile):
        step(tile, True, every, False)

    @pl.loop(full, block)
    def _(tile):
        step(tile, False, every, False)

    step(block, True, range(PIECES // 2), False)
    step(block, True, upper, True)


def stack_heads(rows):
    parts = []
    for half in range(2):
        kept = rows[:, HALF * half : HALF * (half + 1)]
        for h in range(GROUP):
            part = kept[:, :, HEAD_DIM * h : HEAD_DIM * (h + 1)]
            parts.append(part.reshape(SPAN, HEAD_DIM))
    return jnp.concatenate(parts, axis=0)


def unstack_heads(stacked):
    halves = []
    for half in range(2):
        parts = [
            stacked[HALF_ROWS * half + SPAN * h : HALF_ROWS * half + SPAN * (h + 1)]
            for h in range(GROUP)
        ]
        rows = jnp.concatenate(parts + [jnp.zeros_like(parts[0])], axis=1)
        halves.append(rows.reshape(2, HALF, OUT_COLS))
    return jnp.concatenate(halves, axis=1)


def pad_halves(rows):
    gap = jnp.zeros((QPAD // 2 - HALF_ROWS, rows.shape[1]), rows.dtype)
    return jnp.concatenate([rows[:HALF_ROWS], gap, rows[HALF_ROWS:], gap], axis=0)


def skip_gaps(rows):
    return jnp.concatenate([rows[:HALF_ROWS], rows[QPAD // 2 : QPAD // 2 + HALF_ROWS]], axis=0)


PIECE = 512
PIECES = TILE // PIECE


def seen(places, lowest, highest, first):
    times = [whole // part for whole, part in zip(places.shape, lowest.shape)]

    def spread_out(rows):
        for axis, count in enumerate(times):
            if count > 1:
                rows = jnp.concatenate([rows] * count, axis=axis)
        return rows

    return (places <= spread_out(highest - first)) & (places >= spread_out(lowest - first))


def attend_kernel(
    starts_ref,
    chip_ref,
    q_ref,
    kv_first,
    kv_second,
    kv_third,
    mixed_ref,
    out_ref,
    lse_ref,
    keys_out,
    turned_out,
    m_ref,
    acc_ref,
    values_ref,
    turned_ref,
):
    block = pl.program_id(0)
    for (order, first, count), kv in zip(KEY_SPLITS, (kv_first, kv_second, kv_third)):
        first, count = first // (2 * SPAN), count // (2 * SPAN)

        @pl.when((block >= first) & (block < first + count))
        def _(order=order, kv=kv):
            lane = lax.broadcasted_iota(jnp.int32, (HALF_TILE, 2 * HEAD_DIM), 1)
            none = jnp.zeros((HEAD_DIM, HALF_TILE), bf16)
            for half in range(2):
                at = pl.ds(SPAN * half, SPAN)
                keys = jnp.concatenate([kv[(*spot, at)] for spot in natural(order[::-1])], axis=0)
                turned = jnp.concatenate([keys.T[:HEAD_DIM], none], axis=0)
                keys_out[half] = keys
                turned_out[half] = turned
                turned_ref[2 * block + half] = turned
                values_ref[2 * block + half] = jnp.where(lane < HEAD_DIM, jnp.ones_like(keys), keys)

    m_ref[...] = jnp.full(m_ref.shape, masked_score, f32)
    acc_ref[...] = jnp.zeros(acc_ref.shape, f32)
    query = stack_heads(q_ref[...].astype(f32)).astype(bf16)
    row = lax.broadcasted_iota(jnp.int32, query.shape, 0)
    lane = lax.broadcasted_iota(jnp.int32, query.shape, 1)
    slot = (row & (SPAN - 1)) + jnp.where(row >= HALF_ROWS, SPAN, 0)
    query = jnp.concatenate([query, jnp.where(slot == lane, 1.0, 0.0).astype(bf16)], axis=1)
    none = jnp.zeros((HEAD_DIM - 2 * SPAN, PIECE), bf16)
    places = key_places((2 * SPAN, PIECE), 1)
    pos = query_places(block, chip_ref, (2 * SPAN, 128), 0)
    start = begins(starts_ref, pos)

    def tile_step(tile, masked, pieces, upper):
        rows = pl.ds(HALF_ROWS, HALF_ROWS) if upper else pl.ds(0, QROWS)
        asked = query[HALF_ROWS:] if upper else query
        found = []
        for piece in pieces:
            half, at = 2 * tile + piece // 2, pl.ds(piece % 2 * PIECE, PIECE)
            if masked:
                allowed = seen(places, start, pos, first_place(tile, piece))
                table = jnp.where(allowed, 0.0, masked_score).astype(bf16)
                keys = jnp.concatenate([turned_ref[half, pl.ds(0, HEAD_DIM), at], table, none], axis=0)
            else:
                keys = turned_ref[half, :, at]
            found.append(mm(asked, keys, NN))
        before = m_ref[rows]
        highest = found[0]
        for scores in found[1:]:
            highest = jnp.maximum(highest, scores)
        highest = jnp.max(highest, axis=1, keepdims=True)
        highest = jnp.maximum(before, jnp.broadcast_to(highest, before.shape))
        m_ref[rows] = highest
        total = acc_ref[rows] * jnp.exp(before - highest)
        level = jnp.concatenate([highest] * (PIECE // 128), axis=1)
        for piece, scores in zip(pieces, found):
            weights = jnp.exp(scores - level).astype(bf16)
            values = values_ref[2 * tile + piece // 2, pl.ds(piece % 2 * PIECE, PIECE)]
            total = total + mm(weights, values, NN)
        acc_ref[rows] = total

    over_tiles(block, starts_ref, chip_ref, tile_step)
    total = jnp.broadcast_to(acc_ref[:, 0:1], acc_ref.shape)
    out = acc_ref[...] / total
    out_ref[0] = pad_halves(out)
    mixed_ref[...] = unstack_heads(out[:, HEAD_DIM:]).astype(bf16)
    lse_ref[0] = pad_halves(m_ref[...] + jnp.log(total)).T[0:8]


def row_block(lanes):
    return pl.BlockSpec((2, SPAN, lanes), lambda b, *_: (0, b, 0))


def one_block(rows, lanes):
    return pl.BlockSpec((1, rows, lanes), lambda b, *_: (b, 0, 0))


def two_halves(rows, lanes):
    return pl.BlockSpec((2, rows, lanes), lambda b, *_: (b, 0, 0))


def tile_block(first, count):
    first, count = first // (2 * SPAN), count // (2 * SPAN)
    return pl.BlockSpec(
        (RING, RING, RING, 2 * SPAN, 2 * HEAD_DIM),
        lambda b, *_: (0, 0, 0, jnp.clip(b - first, 0, count - 1), 0),
    )


def whole(*shape):
    return pl.BlockSpec(shape, lambda b, *_: (0,) * len(shape))


def attend(starts, chip, query, *keys):
    pairs = BLOCKS * 2 * QROWS * TILE
    return pl.pallas_call(
        attend_kernel,
        out_shape=[
            jax.ShapeDtypeStruct((2, LOCAL, OUT_COLS), bf16),
            jax.ShapeDtypeStruct((BLOCKS, QPAD, 2 * HEAD_DIM), f32),
            jax.ShapeDtypeStruct((BLOCKS, 8, QPAD), f32),
            jax.ShapeDtypeStruct((2 * BLOCKS, HALF_TILE, 2 * HEAD_DIM), bf16),
            jax.ShapeDtypeStruct((2 * BLOCKS, 2 * HEAD_DIM, HALF_TILE), bf16),
        ],
        grid_spec=pltpu.PrefetchScalarGridSpec(
            num_scalar_prefetch=2,
            grid=(BLOCKS,),
            in_specs=[row_block(OUT_COLS), *(tile_block(*split[1:]) for split in KEY_SPLITS)],
            out_specs=[
                row_block(OUT_COLS),
                one_block(QPAD, 2 * HEAD_DIM),
                one_block(8, QPAD),
                two_halves(HALF_TILE, 2 * HEAD_DIM),
                two_halves(2 * HEAD_DIM, HALF_TILE),
            ],
            scratch_shapes=[
                VM((QROWS, 2 * HEAD_DIM), f32),
                VM((QROWS, 2 * HEAD_DIM), f32),
                VM((2 * BLOCKS, HALF_TILE, 2 * HEAD_DIM), bf16),
                VM((2 * BLOCKS, 2 * HEAD_DIM, HALF_TILE), bf16),
            ],
        ),
        compiler_params=pltpu.CompilerParams(
            dimension_semantics=("arbitrary",), vmem_limit_bytes=56 << 20
        ),
        cost_estimate=pl.CostEstimate(
            flops=pairs * 512, bytes_accessed=5 << 20, transcendentals=pairs
        ),
    )(starts, chip, query, *keys)


def three_terms(numbers):
    first = numbers.astype(bf16)
    rest = numbers - first.astype(f32)
    second = rest.astype(bf16)
    third = (rest - second.astype(f32)).astype(bf16)
    return jnp.concatenate([first, second, third], axis=0)


def attend_back_kernel(
    starts_ref,
    chip_ref,
    q_ref,
    branch_ref,
    six_ref,
    last_ref,
    keys_in,
    turned_in,
    out_ref,
    lse_ref,
    dq_ref,
    dkv_first,
    dkv_second,
    dkv_third,
    keys_ref,
    turned_ref,
    sum_ref,
    delta_ref,
    dq_acc,
):
    block = pl.program_id(0)
    own = pl.ds(2 * block, 2)
    keys_ref[own] = keys_in[...]
    turned_ref[own] = turned_in[...]
    sum_ref[own] = jnp.zeros((2, HALF_TILE, 2 * HEAD_DIM), f32)

    @pl.when(block == 0)
    def _():
        branch = branch_ref[...].reshape(CHIP, WIDE)
        delta = mm(branch, six_ref[...], NN)
        delta_ref[:, :, pl.ds(0, HEADS_6)] = delta.astype(bf16).reshape(2, LOCAL, HEADS_6)
        delta = mm(branch, last_ref[...], NN)
        delta_ref[:, :, pl.ds(HEADS_6, 128)] = delta.astype(bf16).reshape(2, LOCAL, 128)

    dq_acc[...] = jnp.zeros(dq_acc.shape, f32)
    mine = pl.ds(pl.multiple_of(block * SPAN, SPAN), SPAN)
    query = pad_halves(stack_heads(q_ref[...].astype(f32)).astype(bf16))
    delta_out = pad_halves(stack_heads(delta_ref[:, mine, :].astype(f32)).astype(bf16))
    none = jnp.zeros_like(query)
    delta_out = jnp.concatenate([none, delta_out], axis=1)
    both = jnp.concatenate([jnp.concatenate([query, none], axis=1), delta_out], axis=0)
    inner = jnp.sum((delta_out.astype(f32) * out_ref[0]).T, axis=0, keepdims=True)
    slot = lax.broadcasted_iota(jnp.int32, (2 * SPAN, 2 * QPAD), 0)
    lane = lax.broadcasted_iota(jnp.int32, (2 * SPAN, 2 * QPAD), 1)
    within = lane & (QPAD // 2 - 1)
    asked = (within & (SPAN - 1)) + ((lane >> 7) & 1) * SPAN
    which = (asked == slot) & (within < HALF_ROWS) & (lane < QPAD)
    which = jnp.where(which, 1.0, 0.0).astype(bf16)
    taken = three_terms(jnp.concatenate([-lse_ref[0, 0:1], -inner], axis=1))
    rest = jnp.zeros((2 * HEAD_DIM - 2 * SPAN - 3, 2 * QPAD), bf16)
    both_turned = jnp.concatenate([both.T, which, taken, rest], axis=0)
    half = QPAD // 2
    upper_turned = jnp.concatenate(
        [both_turned[:, half:QPAD], both_turned[:, QPAD + half :]], axis=1
    )
    upper_both = jnp.concatenate([both[half:QPAD], both[QPAD + half :]], axis=0)
    lane = lax.broadcasted_iota(jnp.int32, (PIECE, 2 * HEAD_DIM), 1)
    ones = jnp.where((lane >= 2 * SPAN) & (lane < 2 * SPAN + 3), 1.0, 0.0)
    places = key_places((PIECE, 2 * HEAD_DIM), 0)
    pos = query_places(block, chip_ref, (8, 2 * HEAD_DIM), 1)
    start = begins(starts_ref, pos)
    slot_lane = lax.broadcasted_iota(jnp.int32, pos.shape, 1) < 2 * SPAN
    far = jnp.int32(1 << 20)
    pos, start = jnp.where(slot_lane, pos, far), jnp.where(slot_lane, start, -far)

    def tile_step(tile, masked, pieces, upper):
        turned, rows = (upper_turned, upper_both) if upper else (both_turned, both)
        lanes = pl.ds(half, half) if upper else pl.ds(0, QPAD)
        width = half if upper else QPAD

        def product(piece):
            keys = keys_ref[2 * tile + piece // 2, pl.ds(piece % 2 * PIECE, PIECE)]
            beside = ones
            if masked:
                allowed = seen(places, start, pos, first_place(tile, piece))
                beside = jnp.where(allowed, ones, masked_score)
            return mm(jnp.concatenate([keys, beside.astype(bf16)], axis=1), turned, NN)

        ahead = product(pieces[0])
        total = dq_acc[:, lanes]
        for piece in pieces:
            raw = ahead
            if piece + 1 in pieces:
                ahead = product(piece + 1)
            scores, delta = raw[:, :width], raw[:, width:]
            weights = jnp.exp(scores)
            delta = (weights * delta).astype(bf16)
            joined = jnp.concatenate([delta, weights.astype(bf16)], axis=1)
            at = pl.ds(piece % 2 * PIECE, PIECE)
            sum_ref[2 * tile + piece // 2, at] += mm(joined, rows, NN)
            total = total + mm(turned_ref[2 * tile + piece // 2, :, at], delta, NN)
        dq_acc[:, lanes] = total

    over_tiles(block, starts_ref, chip_ref, tile_step)
    delta_q = skip_gaps(dq_acc[...].T)[:, :HEAD_DIM] * HEAD_DIM ** (-0.5)
    dq_ref[...] = unstack_heads(delta_q)

    @pl.when(block == BLOCKS - 1)
    def _():
        for (order, first, count), dkv in zip(ROW_SPLITS, (dkv_first, dkv_second, dkv_third)):

            @pl.loop(0, count // SPAN)
            def _(number, order=order, first=first, dkv=dkv):
                at = pl.ds(pl.multiple_of(number * SPAN, SPAN), SPAN)
                sums = sum_ref[first // SPAN + number].astype(bf16)
                for chip, spot in enumerate(natural(order)):
                    dkv[(*spot, at)] = sums[SPAN * chip : SPAN * (chip + 1)]


def attend_back(starts, chip, query, branch, att, keys, turned, out, lse):
    pairs = BLOCKS * 2 * QROWS * TILE
    sums = [(RING, RING, RING, count, 2 * HEAD_DIM) for _, _, count in ROW_SPLITS]
    return pl.pallas_call(
        attend_back_kernel,
        out_shape=[
            jax.ShapeDtypeStruct((2, LOCAL, OUT_COLS), f32),
            *(jax.ShapeDtypeStruct(shape, bf16) for shape in sums),
        ],
        grid_spec=pltpu.PrefetchScalarGridSpec(
            num_scalar_prefetch=2,
            grid=(BLOCKS,),
            in_specs=[
                row_block(OUT_COLS),
                whole(2, LOCAL, WIDE),
                pl.BlockSpec((WIDE, HEADS_6), lambda b, *_: (0, 1)),
                pl.BlockSpec((WIDE, 128), lambda b, *_: (0, LAST // 128)),
                two_halves(HALF_TILE, 2 * HEAD_DIM),
                two_halves(2 * HEAD_DIM, HALF_TILE),
                one_block(QPAD, 2 * HEAD_DIM),
                one_block(8, QPAD),
            ],
            out_specs=[row_block(OUT_COLS), *(whole(*shape) for shape in sums)],
            scratch_shapes=[
                VM((2 * BLOCKS, HALF_TILE, 2 * HEAD_DIM), bf16),
                VM((2 * BLOCKS, 2 * HEAD_DIM, HALF_TILE), bf16),
                VM((2 * BLOCKS, HALF_TILE, 2 * HEAD_DIM), f32),
                VM((2, LOCAL, OUT_COLS), bf16),
                VM((2 * HEAD_DIM, QPAD), f32),
            ],
        ),
        compiler_params=pltpu.CompilerParams(
            dimension_semantics=("arbitrary",), vmem_limit_bytes=56 << 20
        ),
        cost_estimate=pl.CostEstimate(
            flops=pairs * 1280, bytes_accessed=12 << 20, transcendentals=pairs
        ),
    )(starts, chip, query, branch, att, att, keys, turned, out, lse)


def feed_kernel(
    mixed_ref,
    att_ref,
    x_ref,
    gains_ref,
    gate_ref,
    down_ref,
    up_ref,
    wide_ref,
    pack_ref,
    mid_ref,
    dmid_ref,
    both_ref,
    dgain_ref,
    part_ref,
    grad_gate_ref,
    grad_down_ref,
    w_out,
    x_own,
    gate,
    down,
    up,
    wide,
    pack,
    given,
    other,
    normed,
    delta_all,
    hidden_all,
    dn,
    pair_in,
    reduced,
    inbox,
    own_sum,
    w_down,
    w_down_wide,
    send,
    recv,
):
    x, c = lax.axis_index("x"), lax.axis_index("c")
    sibling = step_along("c", 1)
    sems = Sems(send, recv)
    first = [
        sems.fetch(att_ref.at[:, pl.ds(HEADS_6, HEADS_6)], w_out.at[:, pl.ds(0, HEADS_6)]),
        sems.fetch(att_ref.at[:, pl.ds(LAST, 128)], w_out.at[:, pl.ds(HEADS_6, 128)]),
        sems.fetch(x_ref.at[c], x_own),
    ]
    later = [
        sems.fetch(down_ref, down),
        sems.fetch(pack_ref, pack),
        sems.fetch(wide_ref, wide),
        sems.fetch(gate_ref, gate),
        sems.fetch(up_ref, up),
    ]
    greet(axis_peers("xc"))
    for copy in first:
        copy.wait()

    given[...] = mm(mixed_ref[1 - c], w_out[...], NT)
    swap = sems.copy(given, other, sibling)
    swap.start()
    mid = x_own[...].astype(f32) + mm(mixed_ref[c], w_out[...], NT)
    swap.wait()
    mid = mid + other[...]
    mid_ref[...] = mid
    normed[x, c] = (mid * inverse_norm(mid) * gains_ref[1:2]).astype(bf16)
    start_line, own_pair, relay, right_pair, relay_far, far_pair, close_line = gather_line(sems, normed)
    arrivals = (own_pair, relay, right_pair, far_pair)
    start_line()
    for copy in later:
        copy.wait()
    w_down[...] = mm(pack[...], down[...], NN).astype(bf16)
    w_down_wide[...] = mm(w_down[...], wide[...], NN).astype(bf16)

    deltas = (0, 3, 1, 2)
    swaps = [
        sems.copy(dn.at[shifted("x", d), 1 - c], pair_in.at[k], sibling)
        for k, d in enumerate(deltas)
    ]
    sends = [
        sems.copy(reduced.at[k], inbox.at[k], step_along("x", deltas[k + 1])) for k in range(3)
    ]

    def finish(k):
        swaps[k].wait_recv()
        total = dn[shifted("x", deltas[k]), c].astype(f32) + pair_in[k].astype(f32)
        if k == 0:
            own_sum[...] = total
        else:
            reduced[k - 1] = total.astype(bf16)
            sends[k - 1].start()

    def chunk(at):
        rows = normed[at].reshape(CHIP, WIDE)
        joined = mm(rows, gate[...], NN)
        gate_part, above = joined[:, :HID], joined[:, HID:]
        sig = 1.0 / (1.0 + jnp.exp(-gate_part))
        silu = gate_part * sig
        hidden = (silu * above).astype(bf16)
        hidden_all[at] = hidden
        delta = mm(up[at].reshape(CHIP, D), w_down[...], NT)
        delta_gate = (delta * above * sig * (1.0 + gate_part * (1.0 - sig))).astype(bf16)
        delta_above = (delta * silu).astype(bf16)
        delta_all[at, :, pl.ds(0, HID)] = delta_gate
        delta_all[at, :, pl.ds(HID, HID)] = delta_above
        dn[at] = mm(delta_all[at], gate[...], NT).astype(bf16).reshape(2, LOCAL, WIDE)
        part_ref[at] = mm(hidden, w_down_wide[...], NN).astype(bf16).reshape(2, LOCAL, WIDE)

    @pl.loop(0, RING)
    def _(step):
        for k in range(RING):

            @pl.when(step == k)
            def _(k=k):
                arrivals[k]()

        delta = jnp.where(step == 1, 3, jnp.where(step > 1, step - 1, 0))
        chunk(lax.rem(x + delta, RING))
        for k in range(RING):

            @pl.when(step == k)
            def _(k=k):
                swaps[k].start()
                if k == 2:
                    relay_far()
                if k:
                    finish(k - 1)

    finish(3)
    close_line()

    @pl.loop(0, RING)
    def _(block):
        at = pl.ds(pl.multiple_of(block * 256, 256), 256)
        total = jnp.zeros((256, 2 * HID), f32)
        for chip in range(RING):
            total = total + mm(normed[chip, :, :, at].reshape(CHIP, 256), delta_all[chip], TN)
        grad_gate_ref[at, :] = total.astype(bf16)

    total = jnp.zeros((HID, D), f32)
    for chip in range(RING):
        total = total + mm(hidden_all[chip], up[chip].reshape(CHIP, D), TN)
    grad_down_ref[...] = mm(pack[...], total.astype(bf16), TN).astype(bf16)

    for copy in sends:
        copy.wait_recv()
    delta = own_sum[...] + inbox[0].astype(f32) + inbox[1].astype(f32) + inbox[2].astype(f32)
    mid = mid_ref[...]
    scale = inverse_norm(mid)
    dgain_ref[...] = jnp.sum(delta * mid * scale, axis=0, keepdims=True)
    upstream = mm(up[x, c], wide[...], NN)
    dmid = upstream + norm_back(mid, scale, delta, gains_ref[1:2])
    dmid_ref[...] = dmid
    both_ref[c] = dmid.astype(bf16)
    share = sems.copy(both_ref.at[c], both_ref.at[c], sibling)
    share.start()
    for copy in swaps + sends:
        copy.wait_send()
    share.wait()


def feed(mixed, att, x_wide, gains, gate, down, up, widen, pack):
    block = (LOCAL, WIDE)
    return remote_call(
        feed_kernel,
        [
            (block, f32, VM),
            (block, f32, VM),
            ((2, *block), bf16, VM),
            ((1, WIDE), f32, VM),
            ((RING, 2, *block), bf16, VM),
            ((WIDE, 2 * HID), bf16, VM),
            ((16 * DOWN_PAD, D), bf16, VM),
        ],
        [VM, ANY, ANY, VM, ANY, ANY, ANY, ANY, ANY],
        [
            VM((WIDE, OUT_COLS), bf16),
            VM(block, bf16),
            VM((WIDE, 2 * HID), bf16),
            VM((16 * DOWN_PAD, D), bf16),
            VM((RING, 2, LOCAL, D), bf16),
            VM((D, WIDE), bf16),
            VM((HID, 16 * DOWN_PAD), bf16),
            VM(block, f32),
            VM(block, f32),
            VM((RING, 2, *block), bf16),
            VM((RING, CHIP, 2 * HID), bf16),
            VM((RING, CHIP, HID), bf16),
            VM((RING, 2, *block), bf16),
            VM((RING, *block), bf16),
            VM((3, *block), bf16),
            VM((3, *block), bf16),
            VM(block, f32),
            VM((HID, D), bf16),
            VM((HID, WIDE), bf16),
        ],
        32,
        2,
        mixed,
        att,
        x_wide,
        gains,
        gate,
        down,
        up,
        widen,
        pack,
    )


DOWN_SPLITS = (("yz", 0, 32), ("zy", 32, 16))


def settle_kernel(
    dkv_first,
    dkv_second,
    dkv_third,
    dq_ref,
    cos_ref,
    sin_ref,
    normed_ref,
    x_ref,
    mixed_ref,
    both_ref,
    att_ref,
    gains_ref,
    dgain_ref,
    gate_ref,
    down_ref,
    part_ref,
    mid_ref,
    dmid_ref,
    wide_ref,
    turn_ref,
    swap_ref,
    output_ref,
    input_grad_ref,
    in_out,
    out_out,
    gains_out,
    gate_out,
    down_out,
    norm_out,
    *rest,
):
    (send, recv), rest = rest[-2:], list(rest[:-2])
    y, z, x, c = (lax.axis_index(axis) for axis in ALL)
    me = device_number()
    sibling = step_along("c", 1)
    target = lax.rem(me, 8) * 16 + me // 8
    source_of = lax.rem(me, 16) * 8 + me // 16
    line = line_peers()
    sems = Sems(send, recv)

    def pop(count):
        taken = rest[:count]
        del rest[:count]
        return taken

    names = ("one", "two", "three", "normed", "both", "mixed", "xs", "att", "part", "down", "gate", "wide")
    kept = dict(zip(names, pop(len(names))))
    sources = (dkv_first, dkv_second, dkv_third, normed_ref, both_ref, mixed_ref, x_ref, att_ref)
    sources += (part_ref, down_ref, gate_ref, wide_ref)
    fetches = {name: sems.fetch(src, kept[name]) for name, src in zip(names, sources)}
    kv_sum, du_all, du_in, att_own, gate_own, down_own = pop(6)
    att_terms = pop(6)
    pair_in, part_own, part_sum, att_pair, gate_in, slots_line, slots = pop(7)
    deal_refs = [pop(4), pop(4)]
    plane = [
        {"y": lax.rem(y + dy, RING), "z": lax.rem(z + dz, RING)}
        for dy in range(RING)
        for dz in range(RING)
        if dy or dz
    ]
    greet(line + plane, target, source_of)

    def reduce_rows(split, dkv, scratch):
        order, first, count = split
        yield from chip_reduce(sems, order, lambda i: dkv.at[i], scratch)
        kv_sum[pl.ds(first, count), :] = scratch[-1][...]

    def advance(*steps):
        for step in steps:
            next(step, None)

    dkvs = [kept[name] for name in names[:3]]
    for name in names[:3]:
        fetches[name].wait()
    rows = [reduce_rows(split, dkv, pop(10)) for split, dkv in zip(ROW_SPLITS, dkvs)]
    advance(*rows)

    def reduce_down(order, first, count, scratch):
        def view(i):
            at = {"y": slice(None), "z": slice(None), order[0]: i}
            return kept["down"].at[at["y"], at["z"], pl.ds(first, count)]

        yield from chip_reduce(sems, order, view, scratch)
        down_own[pl.ds(first, count), :] = scratch[-1][...]

    def reduce_parts(scratch):
        swaps = [sems.copy(kept["part"].at[i, 1 - c], pair_in.at[i], sibling) for i in range(RING)]
        for swap in swaps:
            swap.start()
        yield
        for i in range(RING):
            swaps[i].wait()
            total = kept["part"][i, c].astype(f32) + pair_in[i].astype(f32)
            part_own[i] = total.astype(bf16).reshape(RING, LOCAL // RING, WIDE)
        yield from reduce_ring(sems, "x", lambda i: part_own.at[i], scratch[:5], scratch[5])
        part_sum[...] = scratch[5][...].reshape(LOCAL, WIDE)

    def reduce_att(split, terms, scratch):
        _, first, lanes = split
        yield from chip_reduce(sems, split[0], lambda i: terms.at[i], scratch)
        att_own[:, :, pl.ds(first, lanes)] = scratch[-1][...].reshape(2, 8, lanes)

    def put_terms(split, buf, terms):
        terms = terms.astype(bf16)
        for chip, spot in enumerate(natural(split[0])):
            buf[spot] = terms[16 * chip : 16 * (chip + 1)]

    cosine, sine = cos_ref[...], sin_ref[...]

    def unrotate(values):
        return (values * cosine - roll_halves(values) * sine).astype(bf16)

    delta_q = dq_ref[...].reshape(CHIP, OUT_COLS)
    early = [unrotate(delta_q[:, 128 * tile : 128 * (tile + 1)]) for tile in range(4)]
    early_six = jnp.concatenate(early[:3], axis=1)
    for name in ("normed", "both", "mixed", "att", "xs"):
        fetches[name].wait()
    grad_in = mm(kept["normed"][...], early_six, TN)
    mixed = kept["mixed"][...].reshape(CHIP, OUT_COLS)
    grad_out = mm(kept["both"][...].reshape(CHIP, WIDE), mixed, TN)
    grad_early = jnp.concatenate([grad_in, grad_out[:, :HEADS_6]], axis=1)
    early_terms, late_terms = att_terms[:3], att_terms[3:]
    for split, buf in zip(EARLY_SPLITS, early_terms):
        put_terms(split, buf, grad_early[:, split[1] : split[1] + split[2]])
    earlies = [
        reduce_att(split, buf, pop(10)) for split, buf in zip(EARLY_SPLITS, early_terms)
    ]
    advance(*earlies)
    advance(*rows)
    fetches["part"].wait()
    fetches["down"].wait()
    parts = reduce_parts(pop(6))
    downs = [reduce_down(*split, pop(8)) for split in DOWN_SPLITS]
    advance(parts, *downs)
    delta_normed = mm(early_six, kept["att"][:, :HEADS_6], NT)
    inputs = kept["xs"][...].reshape(CHIP, WIDE).astype(f32)
    scale = inverse_norm(inputs)
    advance(*rows)
    fetches["gate"].wait()
    gate_sum = kept["gate"][0].astype(f32)
    for number in range(1, 16):
        gate_sum = gate_sum + kept["gate"][number].astype(f32)
    gate_own[...] = gate_sum.reshape(RING, 2, 8, 2 * HID)
    shares = [sems.copy(gate_own.at[peer["x"], peer["c"]], gate_in.at[x, c], peer) for peer in line]
    for copy in shares:
        copy.start()
    gate_in[x, c] = gate_own[x, c]
    advance(*rows)
    advance(*earlies, parts)
    together(*rows)

    sums = [
        kv_sum[pl.ds(SPAN * number + 8 * core, 8)] for core in range(2) for number in range(SPAN)
    ]
    sums = jnp.concatenate(sums, axis=0)
    last = jnp.concatenate([delta_q[:, HEADS_6:HALF_Q], sums[:, :HEAD_DIM]], axis=1)
    delta_v = sums[:, HEAD_DIM:].astype(bf16)
    late = jnp.concatenate([unrotate(last), delta_v, jnp.zeros_like(delta_v)], axis=1)
    grad_late = mm(kept["normed"][...], late, TN)
    put_terms(LATE_SPLITS[0], late_terms[0], grad_late[:, :128])
    put_terms(LATE_SPLITS[1], late_terms[1], grad_late[:, 128:])
    lates = [reduce_att(split, buf, pop(6)) for split, buf in zip(LATE_SPLITS, late_terms)]
    advance(*lates[:2])
    delta_normed = delta_normed + mm(late, kept["att"][:, LATE:LAST], NT)
    gain_one = jnp.sum(delta_normed * (inputs * scale), axis=0, keepdims=True)
    row = lax.broadcasted_iota(jnp.int32, (128, WIDE), 0)
    at_gain = GAIN_AT - LAST
    gain_sums = jnp.where(row == at_gain, gain_one, jnp.where(row == at_gain + 1, dgain_ref[...], 0.0))
    put_terms(LATE_SPLITS[2], late_terms[2], grad_out[:, HEADS_6:] + gain_sums.T)
    advance(lates[2])
    du_all[...] = norm_back(inputs, scale, delta_normed, gains_ref[0:1]).reshape(2, LOCAL, WIDE)
    swap = sems.copy(du_all.at[1 - c], du_in, sibling)
    swap.start()
    advance(*downs, *earlies, parts)
    advance(*lates)

    fetches["wide"].wait()
    widen = kept["wide"]

    def deal_back(values, out, held, first, given, taken):
        values = mm(values, widen[...], NN).astype(bf16)
        yield from deal_line(sems, values, first, turn_ref, held)
        yield from deal_plane(sems, first, out, turn_ref, swap_ref, given, taken)

    together(parts)
    result = (mid_ref[...] + part_sum[...]).astype(bf16)
    output = deal_back(result, output_ref, *deal_refs[0])
    advance(output)
    swap.wait()
    input_grad = (dmid_ref[...] + (du_all[c] + du_in[...])).astype(bf16)
    input_back = deal_back(input_grad, input_grad_ref, *deal_refs[1])
    advance(input_back)
    together(*lates, *earlies, *downs, output, input_back)

    pair = sems.copy(att_own.at[1 - c], att_pair.at[c], sibling)
    pair.start()
    move = sems.copy(down_own, down_out, place(target))
    stay = sems.local(down_own, down_out)

    @pl.when(target != me)
    def _():
        move.start()

    @pl.when(target == me)
    def _():
        stay.start()

    lane = lax.broadcasted_iota(jnp.int32, (16, ATT_COLS), 1)
    is_gain = (lane >= GAIN_AT) & (lane < GAIN_AT + 2)
    att = att_own[...].reshape(16, ATT_COLS)
    gate_sum, down_sum = gate_own[...], down_own[...]
    squares = jnp.sum(jnp.where(is_gain, 0.0, att * att))
    squares = squares + jnp.sum(gate_sum * gate_sum) + jnp.sum(down_sum * down_sum)
    mine = slots_line.at[x, c]
    mine[0] = jnp.where(is_gain, att, 0.0)[:, LAST:]
    mine[1] = jnp.full((16, 128), 1.0, f32) * squares
    copies = [sems.copy(mine, mine, peer) for peer in line]
    for copy in copies:
        copy.start()
    for copy in copies:
        copy.wait()
    total = jnp.zeros((8, 128), f32)
    for i in range(RING):
        gain = slots_line[i, 0, 0] + slots_line[i, 1, 0]
        total = total + (slots_line[i, 0, 1, 0:8] + slots_line[i, 1, 1, 0:8]) + jnp.sum(gain * gain)
    mine = slots.at[y, z]
    mine[...] = total
    copies = [sems.copy(mine, mine, peer) for peer in plane]
    for copy in copies:
        copy.start()
    for copy in copies:
        copy.wait()
    total = slots[0, 0]
    for number in range(1, RING * RING):
        total = total + slots[number // RING, number % RING]
    norm_out[...] = jnp.sqrt(total)

    for copy in shares:
        copy.wait()
    gate_pieces = [gate_in[rank // 2, rank % 2] for rank in range(RANKS)]
    gate_out[...] = jnp.concatenate(
        [piece[:, :SLICE] for piece in gate_pieces]
        + [piece[:, HID : HID + SLICE] for piece in gate_pieces],
        axis=1,
    )
    att_pair[c] = att_own[c]
    pair.wait()
    one, two = att_pair[0], att_pair[1]
    k_at, v_at = LATE + HEAD_DIM, LATE + 2 * HEAD_DIM
    in_out[...] = jnp.concatenate(
        [
            one[:, :HEADS_6],
            one[:, LATE:k_at],
            two[:, :HEADS_6],
            two[:, LATE:k_at],
            one[:, k_at:v_at],
            two[:, k_at:v_at],
            one[:, v_at : v_at + HEAD_DIM],
            two[:, v_at : v_at + HEAD_DIM],
        ],
        axis=1,
    )
    out_out[...] = jnp.concatenate(
        [one[:, HEADS_6:LATE], one[:, LAST:GAIN_AT], two[:, HEADS_6:LATE], two[:, LAST:GAIN_AT]],
        axis=1,
    )
    gains_out[...] = one[:, LAST:] + two[:, LAST:]

    @pl.when(target != me)
    def _():
        move.wait()

    @pl.when(target == me)
    def _():
        stay.wait()


def settle(*args):
    scratch = [
        *(VM((RING, RING, RING, count, 2 * HEAD_DIM), bf16) for _, _, count in ROW_SPLITS),
        VM((CHIP, WIDE), bf16),
        VM((2, LOCAL, WIDE), bf16),
        VM((2, LOCAL, OUT_COLS), bf16),
        VM((2, LOCAL, WIDE), bf16),
        VM((WIDE, ATT_COLS), bf16),
        VM((RING, 2, LOCAL, WIDE), bf16),
        VM((RING, RING, DOWN_PAD, D), bf16),
        VM((16, RING, 16, 2 * HID), bf16),
        VM((WIDE, D), bf16),
        VM((CHIP, 2 * HEAD_DIM), f32),
        VM((2, LOCAL, WIDE), f32),
        VM((LOCAL, WIDE), f32),
        VM((2, 8, ATT_COLS), f32),
        VM((RING, 2, 8, 2 * HID), f32),
        VM((DOWN_PAD, D), f32),
        *(VM((RING, RING, RING, 16, lanes), bf16) for _, _, lanes in EARLY_SPLITS + LATE_SPLITS),
        VM((RING, LOCAL, WIDE), bf16),
        VM((RING, RING, LOCAL // RING, WIDE), bf16),
        VM((LOCAL, WIDE), f32),
        VM((2, 8, ATT_COLS), f32),
        VM((RING, 2, 8, 2 * HID), f32),
        VM((RING, 2, 2, 16, 128), f32),
        VM((RING, RING, 8, 128), f32),
    ]
    scratch += [
        VM((RING, 2, 16, D), bf16),
        VM((RING, 2, 16, D), bf16),
        VM((2, RING, 32, D), bf16),
        VM((2, RING, 32, D), bf16),
    ] * 2
    for order, _, count in ROW_SPLITS:
        scratch += reduce_scratch(order, (count, 2 * HEAD_DIM))
    for order, _, lanes in EARLY_SPLITS:
        scratch += reduce_scratch(order, (16, lanes))
    block = (RING, LOCAL // RING, WIDE)
    scratch += [VM(block, bf16) for _ in range(5)] + [VM(block, f32)]
    for order, _, count in DOWN_SPLITS:
        scratch += reduce_scratch(order, (count, D))
    for order, _, lanes in LATE_SPLITS:
        scratch += reduce_scratch(order, (16, lanes), ring=False)
    return remote_call(
        settle_kernel,
        [
            ((LOCAL, D), bf16, VM),
            ((LOCAL, D), bf16, VM),
            ((8, 1152), f32, VM),
            ((8, D), f32, VM),
            ((8, 128), f32, VM),
            ((8, 2 * FF), f32, VM),
            ((DOWN_PAD, D), f32, VM),
            ((8, 128), f32, VM),
        ],
        [ANY] * 3 + [VM] * 3 + [ANY] * 5 + [VM] * 2 + [ANY] * 3 + [VM] * 2 + [ANY] + [VM] * 2,
        scratch,
        240,
        3,
        *args,
    )


def adam_step(weight, gradient, moment, square, factor, step_rate):
    gradient = gradient * factor
    moment = beta_first * moment + (1.0 - beta_first) * gradient
    square = beta_second * square + (1.0 - beta_second) * gradient * gradient
    moment_hat = moment / (1.0 - beta_first**STEP)
    square_hat = square / (1.0 - beta_second**STEP)
    updated = weight - step_rate * (
        moment_hat / (jnp.sqrt(square_hat) + adam_eps) + decay_rate * weight
    )
    return (updated, moment, square, updated.astype(bf16))


RATES = (
    matrix_rate * D ** (-0.5),
    matrix_rate * 5 ** (-0.5),
    matrix_rate * D ** (-0.5),
    matrix_rate * FF ** (-0.5),
    gain_rate,
)


def optimize_kernel(norm_ref, in_sum, out_sum, gains_sum, gate_sum, down_sum, *refs):
    states, outs = refs[:17], refs[17:]
    factor = 1.0 / jnp.maximum(norm_ref[0:1, 0:1], 1.0)
    gain_lane = GAIN_AT - LAST
    gains = gains_sum[...][:, gain_lane : gain_lane + 8]
    gains = jnp.concatenate([gains, jnp.zeros((8, 120), f32)], axis=1)
    gains = jnp.concatenate([gains, jnp.zeros((120, 128), f32)], axis=0).T
    sums = (
        in_sum[0:7],
        out_sum[0:7],
        gate_sum[0:7],
        down_sum[0:DOWN_ROWS],
        gains[0:2, 0:7],
    )
    for number, gradient in enumerate(sums):
        weight, moment, square = (ref[...] for ref in states[3 * number : 3 * number + 3])
        news = adam_step(weight, gradient, moment, square, factor, RATES[number])
        for ref, new in zip(outs[4 * number : 4 * number + 4], news):
            ref[...] = new
    for ref, new in zip(outs[20:], states[15:]):
        ref[...] = new[...]
    outs[22][...] = norm_ref[0:1, 0:1]


def optimize(norm, sums, states, rows):
    shapes = []
    for number in range(5):
        shape = states[3 * number].shape
        shapes += [jax.ShapeDtypeStruct(shape, f32)] * 3 + [jax.ShapeDtypeStruct(shape, bf16)]
    shapes += [jax.ShapeDtypeStruct((LOCAL, D), bf16)] * 2 + [jax.ShapeDtypeStruct((1, 1), f32)]
    return pl.pallas_call(
        optimize_kernel,
        out_shape=shapes,
        in_specs=[pl.BlockSpec(memory_space=VM)] * (6 + 17),
        out_specs=[pl.BlockSpec(memory_space=VM)] * 23,
        compiler_params=pltpu.CompilerParams(vmem_limit_bytes=56 << 20),
    )(norm, *sums, *states, *rows)


def rotation_table(doc_place):
    half_dim = HEAD_DIM // 2
    inverse = rope_base ** (-(jnp.arange(half_dim, dtype=f32) * 2.0) / HEAD_DIM)
    angles = doc_place.astype(f32)[:, None] * inverse[None, :]
    cosine, sine = jnp.cos(angles), jnp.sin(angles)
    return jnp.concatenate([cosine] * 4, axis=1), jnp.concatenate([-sine, sine] * 2, axis=1)


def body(
    tokens,
    cotangent,
    lengths,
    in_weight,
    out_weight,
    gate_weight,
    down_weight,
    gains,
    in_first,
    out_first,
    gate_first,
    down_first,
    gains_first,
    in_second,
    out_second,
    gate_second,
    down_second,
    gains_second,
):
    chip = (lax.axis_index("y") * RING + lax.axis_index("z")) * RING + lax.axis_index("x")
    widen, pack, turn, swap = widen_matrix(), pack_matrix(), turn_matrix(), swap_matrix()
    pair, gate_line, down_here, x_line, up_line = spread(
        tokens,
        cotangent,
        in_weight,
        out_weight.T,
        gains,
        gate_weight,
        down_weight,
        turn,
    )
    gate_all = lax.all_gather(gate_line, ("y", "z"), axis=0, tiled=False).reshape(WIDE, 2 * HID)
    down_all = lax.all_gather(down_here, ("y", "z"), axis=0, tiled=False).reshape(16 * DOWN_PAD, D)

    row = jnp.arange(CHIP, dtype=jnp.int32)
    position = (row % LOCAL) * DEVICES + 2 * chip + row // LOCAL
    starts = (jnp.cumsum(lengths) - lengths).astype(jnp.int32)
    begin = jnp.max(jnp.where(position[:, None] >= starts, starts, 0), axis=1)
    cosine, sine = rotation_table(position - begin)
    chip_place = (2 * chip).astype(jnp.int32).reshape(1)

    queries, normed, x_wide, gain_rows, att_all, *keys, up_line = project(
        x_line, up_line, pair, turn, swap, widen, order_matrix(), cosine, sine
    )
    att_flat = att_all.reshape(WIDE, ATT_COLS)
    mixed, mixed_wide, lse, keys, turned = attend(starts, chip_place, queries, *keys)
    middle, delta_middle, branch, gain_two, parts, grad_gate, grad_down = feed(
        mixed, att_flat, x_wide, gain_rows, gate_all, down_all, up_line, widen, pack
    )
    spread_over = dict(split_axis=0, concat_axis=0, tiled=True)
    grad_gate = grad_gate.reshape(16, RING, 16, 2 * HID)
    grad_gate = lax.all_to_all(grad_gate, ("y", "z"), **spread_over)
    delta_q, *delta_kv = attend_back(
        starts, chip_place, queries, branch, att_flat, keys, turned, mixed_wide, lse
    )
    output, input_grad, *sums, norm = settle(
        *delta_kv,
        delta_q,
        cosine,
        sine,
        normed,
        x_wide,
        mixed,
        branch,
        att_flat,
        gain_rows,
        gain_two,
        grad_gate,
        grad_down.reshape(RING, RING, DOWN_PAD, D),
        parts,
        middle,
        delta_middle,
        widen_matrix(turned=True),
        turn,
        swap,
    )

    states = (
        *(in_weight, in_first, in_second),
        *(out_weight.T, out_first.T, out_second.T),
        *(gate_weight, gate_first, gate_second),
        *(down_weight, down_first, down_second),
        *(gains, gains_first, gains_second),
    )
    new = optimize(norm, sums, states, (output, input_grad))
    out_new = [values.T for values in new[4:8]]
    return (*new[20:22], *new[:4], *out_new, *new[8:20], new[22].reshape(()))


def solution(mesh):
    grid = Mesh(mesh.devices.reshape(RING, RING, RING, 2), ALL)
    rows, columns = P(ALL, None), P(None, ALL)
    return jax.shard_map(
        body,
        mesh=grid,
        in_specs=(
            rows,
            rows,
            P(),
            rows,
            columns,
            rows,
            rows,
            columns,
            rows,
            columns,
            rows,
            rows,
            columns,
            rows,
            columns,
            rows,
            rows,
            columns,
        ),
        out_specs=(
            rows,
            rows,
            *[rows] * 4,
            *[columns] * 4,
            *[rows] * 8,
            *[columns] * 4,
            P(),
        ),
        check_vma=False,
    )
```

time: 3290 us -> 324 us (0.10)
  local copies, waits for them, and re-layouts: 1030 us -> 1.5 us
  blocking collectives: 942 us -> 0 us
  waiting for transfers between devices: 445 us -> 0.73 us
  matrix products: 362 us -> 0 us
  Pallas kernels: 0 us -> 297 us
  other arithmetic: 234 us -> 3.12 us
  starting transfers between devices: 220 us -> 5.58 us
    unnamed x3 -> x0, blocking collectives: 847 us -> none
    dynamic_update_slice x4 -> x0, local copies, waits for them, and re-layouts: 398 us -> none  [back_step(): lax.dynamic_update_slice_in_dim(pad_grads, current + both_parts, first_ro...]
    dot_general x40 -> x0, matrix products: 362 us -> none  [the longest x8 115 us: window_scores(): jnp.einsum('qkgd,skd->kgqs', block_query, key_window, preferred_element_t...]
    pallas_call x0 -> x7, Pallas kernels: none -> 297 us  [the longest x4 233 us: remote_call(): pl.pallas_call(kernel, out_shape=[jax.ShapeDtypeStruct(shape, dtype) for...]
    reshape x33 -> x0, local copies, waits for them, and re-layouts: 268 us -> none  [the longest x4 63.6 us: back_step(): value_part.reshape(devices, span_rows, key_width)]
    reduce_scatter x1 -> x0, waiting for transfers between devices: 240 us -> none  [body(): lax.psum_scatter(pad_grads[:, reach_rows:, :].reshape(devices * local_row...]
    all_gather x6 -> x2, waiting for transfers between devices: 180 us -> 0.01 us  [the longest x1 0.01 us: body(): lax.all_gather(gate_line, ('y', 'z'), axis=0, tiled=False)]
    unnamed x154 -> x4, local copies, waits for them, and re-layouts: 182 us -> 1.5 us
  transfers between devices with their start and end apart: 55 -> 3, of which waited for: 8 -> 0; matrix products, arithmetic and copies ran while one was open for 40% -> 1% of each run, Pallas kernels for 0% -> 42%
where the time goes in v1:
time: 324 us; the launch traced here: 322 us
  Pallas kernels  297 us (92%)
  between operations  14.2 us (4%)
  starting transfers between devices  5.58 us (2%)
    pallas_call x4, Pallas kernels, remote_call(): pl.pallas_call(kernel, out_shape=[jax.ShapeDtypeStruct(shape, dtype) for...  233 us
    pallas_call x1, Pallas kernels, attend_back(): pl.pallas_call(attend_back_kernel, out_shape=[jax.ShapeDtypeStruct((2, LO...  35.2 us
    pallas_call x1, Pallas kernels, attend(): pl.pallas_call(attend_kernel, out_shape=[jax.ShapeDtypeStruct((2, LOCAL,...  25.6 us
  transfers between devices with their start and end apart: 3, of which 0 were waited for; matrix products, arithmetic and copies ran while one was open for 1% of the time, Pallas kernels for 42%

profile of v1, /device:TPU:1, one launch (start us, length us, event | category | flops | bytes accessed | tf_op | source)
XLA Modules:
  0.0 322.4 jit_solution(1026313021539855315)
XLA Ops:
  7.2 0.0 all-gather.7.cloned.1.call-start
  7.2 22.4 %shard_map.407 = (bf16[16,1152]{1,0:T(8,128)(2,1)}, bf16[4,16,1280]{2,1,0:T(8,128)(2,1)}, bf16[48,896]{1,0:T(8,128)(2,1)}, bf16[4,2,16,896]{3,2,1,0:T(8,128)(2,1)}, bf16[4,2,16,896]{3,2,1,0:T(8,128)(2,1)}) custom-call(bf16[128,896]{1,0:T(8,128)(2,1)} %tokens_ref.1, bf16[128,896]{1,0:T(8,128)(2,1)} %cotangent_ref.1, f32[7,1152]{1,0:T(8,128)} %refs_0_.1, ...), custom_call_target="tpu_custom_call" | custom-call | tf_op jit(solution)/shard_map/pallas_call | solution.py:378
  29.6 0.0 all-gather.7.cloned.1.call-update
  29.7 0.0 all-gather.5.cloned.1.call-start
  29.7 0.7 all-gather.5.cloned.1.call-update
  30.4 0.8 reduce-window.9
  31.3 0.7 bitcast_subtract_fusion.starts_ref
  31.9 0.0 copy-start.1
  31.9 0.1 select_reduce_fusion
  32.0 0.5 fusion
  32.6 1.0 pad_maximum_fusion
  33.6 74.1 %shard_map.408 = (bf16[2,128,512]{2,1,0:T(8,128)(2,1)}, bf16[256,1024]{1,0:T(8,128)(2,1)}, bf16[2,128,1024]{2,1,0:T(8,128)(2,1)}, f32[8,1024]{1,0:T(8,128)}, bf1...) custom-call(bf16[4,2,16,896]{3,2,1,0:T(8,128)(2,1)} %get-tuple-eleme, ...), custom_call_target="tpu_custom_call" | custom-call | tf_op jit(solution)/shard_map/pallas_call | solution.py:378
  107.6 0.0 copy-done.1
  107.6 25.6 %shard_map.409 = (bf16[2,128,512]{2,1,0:T(8,128)(2,1)}, f32[8,256,128]{2,1,0:T(8,128)}, f32[8,8,256]{2,1,0:T(8,128)}, bf16[16,1024,128]{2,1,0:T(8,128)(2,1)}, bf16[16,128,1024]{2,1,0:T(8,128)(2,1)}) custom-call(s32[6]{0:T(128)} %copy-done.1, s32[1]{0:T(128)} %bitcast.2.chip_ref, bf16[2,128,512]{2,1,0:T(8,128)(2,1)} %get-tuple-element.87.q_ref, ...), custom_call_target="tpu_custom_call" | custom-call | flops 3758096384 | bytes 5242880 | tf_op jit(solution)/shard_map/pallas_call | solution.py:947
  133.2 0.0 all-gather.7.cloned.1.call-done.down_ref
  133.2 0.0 all-gather.5.cloned.1.call-done
  133.2 42.9 %shard_map.410 = (f32[128,1024]{1,0:T(8,128)}, f32[128,1024]{1,0:T(8,128)}, bf16[2,128,1024]{2,1,0:T(8,128)(2,1)}, f32[1,1024]{1,0:T(1,128)}, bf16[4,2,128,1024]...) custom-call(bf16[2,128,512]{2,1,0:T(8,128)(2,1)} %get-tuple-element.91.mixed_ref, ...), custom_call_target="tpu_custom_call" | custom-call | tf_op jit(solution)/shard_map/pallas_call | solution.py:378
  176.2 5.5 %all-to-all-start = ((bf16[16,4,16,1280]{3,2,1,0:T(8,128)(2,1)}), bf16[16,4,16,1280]{3,2,1,0:T(8,128)(2,1)S(1)}, u32[]{:S(2)}, u32[]{:S(2)}) async-start(bf16[16,4,16,1280]{3,2,1,0:T(8,128)(2,1)} %bitcast.20), calls=%async_computation | async-start | bytes 5242880 | tf_op jit(solution)/shard_map/all_to_all | solution.py:1815
  181.7 35.2 %shard_map.411 = (f32[2,128,512]{2,1,0:T(8,128)}, bf16[4,4,4,96,128]{4,3,2,1,0:T(8,128)(2,1)}, bf16[4,4,4,96,128]{4,3,2,1,0:T(8,128)(2,1)}, bf16[4,4,4,64,128]{4,3,2,1,0:T(8,128)(2,1)}) custom-call(s32[6]{0:T(128)} %copy-done.1, s32[1]{0:T(128)} %bitcast.2.chip_ref, bf16[2,128,512]{2,1,0:T(8,128)(2,1)} %get-tuple-element.87.q_ref, ...), custom_call_target="tpu_custom_call" | custom-call | flops 9395240960 | bytes 12582912 | tf_op jit(solution)/shard_map/pallas_call | solution.py:1104
  216.9 0.0 all-to-all-done.gate_ref
  216.9 0.0 copy-start
  216.9 1.5 copy-done
  218.4 93.5 %shard_map.412 = (bf16[128,896]{1,0:T(8,128)(2,1)}, bf16[128,896]{1,0:T(8,128)(2,1)}, f32[8,1152]{1,0:T(8,128)}, f32[8,896]{1,0:T(8,128)}, f32[8,128]{1,0:T(8,12...) custom-call(bf16[4,4,4,96,128]{4,3,2,1,0:T(8,128)(2,1)} %get-tuple-element.103.dkv_first, ...), custom_call_target="tpu_custom_call" | custom-call | tf_op jit(solution)/shard_map/pallas_call | solution.py:378
  311.9 3.7 %shard_map.413 = (f32[7,1152]{1,0:T(8,128)}, f32[7,1152]{1,0:T(8,128)}, f32[7,1152]{1,0:T(8,128)}, bf16[7,1152]{1,0:T(8,128)(2,1)}, f32[7,896]{1,0:T(8,128)}, /*...) custom-call(f32[8,128]{1,0:T(8,128)} %get-tuple-element.114.norm_ref, ...), custom_call_target="tpu_custom_call" | custom-call | tf_op jit(solution)/shard_map/pallas_call | solution.py:1746
  (3 shorter events, 0.0 us)
Async XLA Ops:
  7.2 126.0 %all-gather.7.cloned.1.call-start = ((), (), s32[]{:S(2)}) async-start(), calls=%async_computation.2 | async-start | bytes 1462272 | tf_op jit(solution)/shard_map/all_gather | solution.py:1796
  29.7 103.5 %all-gather.5.cloned.1.call-start = ((), (), s32[]{:S(2)}) async-start(), calls=%async_computation.1 | async-start | bytes 2785280 | tf_op jit(solution)/shard_map/all_gather | solution.py:1795
  31.9 75.7 %copy-start.1 = (s32[6]{0:T(128)}, s32[6]{0:T(128)S(1)}, u32[]{:S(2)}) copy-start(s32[6]{0:T(128)S(1)} %bitcast_subtract_fusion.starts_ref) | copy-start | bytes 76
  176.2 40.7 %all-to-all-start = ((bf16[16,4,16,1280]{3,2,1,0:T(8,128)(2,1)}), bf16[16,4,16,1280]{3,2,1,0:T(8,128)(2,1)S(1)}, u32[]{:S(2)}, u32[]{:S(2)}) async-start(bf16[16,4,16,1280]{3,2,1,0:T(8,128)(2,1)} %bitcast.20), calls=%async_computation | async-start | bytes 5242880 | tf_op jit(solution)/shard_map/all_to_all | solution.py:1815
  216.9 1.5 copy-start
Sparse Core Ops, SparseCore 0:
  29.8 44.3 all-gather.6
  76.3 46.3 all-gather.4
